TPU v7x, 128 devices: a whole 4x4x4 slice. The times are simulated.
128 devices in a mesh: ep: 32 (over y, z, core), tp: 4 (over x).
Axes of the slice: x: 4, y: 4, z: 4, core: 2. Of those that a mesh axis runs over, the one named last changes fastest.
Arguments:
- tokens: bfloat16 [4096, 4096], P('ep', 'tp'), may hold values from -6 to 6
- keep_mask: int32 [4096], P('ep'), may hold values 0 or 1
- expert_ids: int32 [4096, 8], P('ep'), may hold values from 0 to 63, all different within a row; in each aligned block of 128 rows (0 to 127, 128 to 255, ...) at most 32 rows name the same one
- route_weight: float32 [4096, 8], P('ep'), may hold values from 0.1 to 1
- w_gate: bfloat16 [64, 4096, 1536], P('ep', None, 'tp'), may hold values from -0.09375 to 0.09375
- w_up: bfloat16 [64, 4096, 1536], P('ep', None, 'tp'), may hold values from -0.09375 to 0.09375
- w_down: bfloat16 [64, 1536, 4096], P('ep', 'tp'), may hold values from -0.15625 to 0.15625
- norm_gain: float32 [4096], replicated, may hold values from 0.1 to 1.9
- kv_weight: bfloat16 [4096, 1024], P(None, 'tp'), may hold values from -0.09375 to 0.09375
Outputs:
- mixed_out: bfloat16 [4096, 4096], P('ep', 'tp')
- kv_rows: bfloat16 [4096, 1024], P('ep', 'tp')
Inputs may be any that keep to these rules, and one draw needn't show every extreme that they name: `expert_ids`: within the rows of one device (128 rows, aligned blocks) no expert is named by more than 32 rows, a bound that some block reaches; a row names 8 different experts.
All inputs are finite; a program needn't handle non-finite values. No bound on the sum of `keep_mask` on one device may be relied on, other than what follows from the above.
Results may differ from a plain program's by a relative error of at most 0.014.
Values may be sent and summed in bfloat16 or wider, within the bound.
No kernel may reach another device: no remote copies, remote signals or barrier semaphores. Data moves between devices by JAX's collectives and lax.ppermute only.
A program may use at most 128 MiB of HBM per device.

v0:
```python
import functools

import jax
import jax.numpy as jnp
import numpy as np
from jax import lax
from jax.experimental import pallas as pl
from jax.experimental.pallas import tpu as pltpu
from jax.sharding import Mesh, PartitionSpec as P

AXES = ("y", "z", "c", "x")
SIZES = (4, 4, 2, 4)
LINKS = (("x", 1), ("y", 3), ("z", 1), ("x", 3), ("y", 1), ("z", 3))
STAGES = len(LINKS)
PEERS = 1 << STAGES
HALF = PEERS // 2
BLOCKS = 16
TOK = 128
WIDTH = 1024
SLOTS = 32
CHIP_EXPERTS = 4
LANES = 128
TILES = WIDTH // LANES
ROWS = (352, 336, 336)
ROW_AT = (0, 352, 688)
PARTS = len(ROWS)
PAIRS = BLOCKS // 2
GROUPS = 4
SLOT_STEP = SLOTS // GROUPS
GROUP_ROWS = 2 * SLOT_STEP
TILE = PAIRS * GROUP_ROWS
PAIR_ROWS = CHIP_EXPERTS * GROUPS * GROUP_ROWS


def tiles_of(part):
    first, last = ROW_AT[part], ROW_AT[part] + ROWS[part]
    found = []
    for tile in range(first // TOK, -(-last // TOK)):
        start, stop = max(first - tile * TOK, 0), min(last - tile * TOK, TOK)
        found.append((tile, start, stop, tile * TOK + start - first))
    return found


def link_of(part, core, stage):
    return LINKS[(2 * part + core + stage) % STAGES]


def device_number(at):
    return ((at["y"] * 4 + at["z"]) * 2 + at["c"]) * 4 + at["x"]


def all_places():
    for y in range(4):
        for z in range(4):
            for c in range(2):
                for x in range(4):
                    yield dict(y=y, z=z, c=c, x=x)


def stage_pairs(part, stage):
    pairs = []
    for at in all_places():
        axis, mask = link_of(part, at["c"], stage)
        to = dict(at)
        to[axis] ^= mask
        pairs.append((device_number(at), device_number(to)))
    return pairs


def core_pairs():
    return [(device_number(at), device_number(dict(at, c=1 - at["c"]))) for at in all_places()]


def x_pairs(mask):
    return [(device_number(at), device_number(dict(at, x=at["x"] ^ mask))) for at in all_places()]


def place_table():
    place = np.zeros((128, PARTS, BLOCKS * 4), np.int32)
    for at in all_places():
        for part in range(PARTS):
            for j in range(PEERS):
                to = dict(at)
                for stage in range(STAGES):
                    if j >> stage & 1:
                        axis, mask = link_of(part, at["c"], stage)
                        to[axis] ^= mask
                place[device_number(at), part, (to["y"] * 4 + to["z"]) * 4 + to["x"]] = j
    return place.reshape(128, -1)


def hidden_kernel(
    place, groups, pick, weight, lo0, hi0, lo1, hi1, lo2, hi2, g_own, u_own, g_far, u_far,
    out, rows, tok, wide, tok_sems, weight_sems,
):
    low, high = (lo0, lo1, lo2), (hi0, hi1, hi2)
    ff = g_own.shape[2]

    def weight_copies(gate, up, at, slot):
        return (
            pltpu.make_async_copy(gate.at[at], wide.at[slot, :, pl.ds(0, ff)], weight_sems.at[slot, 0]),
            pltpu.make_async_copy(up.at[at], wide.at[slot, :, pl.ds(ff, ff)], weight_sems.at[slot, 1]),
        )

    def fetch(pair, slot, start):
        for blk in range(2):
            for x in range(4):
                for part in range(PARTS):
                    to = tok.at[slot, blk, x, pl.ds(ROW_AT[part], ROWS[part])]
                    sem = tok_sems.at[slot, (blk * 4 + x) * PARTS + part]
                    if not start:
                        pltpu.make_async_copy(low[part].at[0], to, sem).wait()
                        continue
                    j = place[part * PEERS + (2 * pair + blk) * 4 + x]

                    @pl.when(j < HALF)
                    def _(part=part, j=j, to=to, sem=sem):
                        pltpu.make_async_copy(low[part].at[j], to, sem).start()

                    @pl.when(j >= HALF)
                    def _(part=part, j=j, to=to, sem=sem):
                        pltpu.make_async_copy(high[part].at[j - HALF], to, sem).start()

    fetch(0, 0, True)
    for copy in weight_copies(g_own, u_own, 0, 0):
        copy.start()

    @pl.loop(0, PAIRS)
    def _(pair):
        slot = lax.rem(pair, 2)

        @pl.when(pair + 1 < PAIRS)
        def _():
            fetch(pair + 1, 1 - slot, True)

        fetch(pair, slot, False)
        at = pl.multiple_of(pair * GROUP_ROWS, GROUP_ROWS)
        for x in range(4):
            cols = slice(x * WIDTH, (x + 1) * WIDTH)
            held = [
                jnp.concatenate([tok[slot, blk, x, t * TOK : (t + 1) * TOK] for blk in range(2)], axis=0)
                for t in range(TILES)
            ]
            held = jnp.concatenate(held, axis=1)
            picked = jnp.dot(pick[pair], held, preferred_element_type=jnp.float32)
            picked = picked.astype(jnp.bfloat16)
            for e in range(CHIP_EXPERTS):
                for g in range(GROUPS):
                    first = (e * GROUPS + g) * GROUP_ROWS
                    rows[e, pl.ds(g * TILE + at, GROUP_ROWS), cols] = picked[first : first + GROUP_ROWS]

    for copy in weight_copies(g_own, u_own, 1, 1):
        copy.start()

    @pl.loop(0, CHIP_EXPERTS)
    def _(e):
        slot = lax.rem(e, 2)
        for copy in weight_copies(g_own, u_own, 0, slot):
            copy.wait()

        @pl.loop(0, lax.div(groups[e] + 1, 2))
        def _(g):
            for i in range(2):
                tile = pl.ds(pl.multiple_of((2 * g + i) * TILE, TILE), TILE)
                both = jnp.dot(rows[e, tile, :], wide[slot], preferred_element_type=jnp.float32)
                product = jax.nn.silu(both[:, :ff]) * both[:, ff:] * weight[e, tile]
                out[e, tile] = product.astype(jnp.bfloat16)

        @pl.when(e < 2)
        def _():
            for copy in weight_copies(g_far, u_far, e, slot):
                copy.start()


def find_hidden(place, groups, pick, weight, pieces, own, far):
    flat = [half for pair in pieces for half in pair]
    ff = own[0].shape[2]
    n = BLOCKS * SLOTS
    anywhere = pl.BlockSpec(memory_space=pl.ANY)
    vmem = pl.BlockSpec(memory_space=pltpu.VMEM)
    smem = pl.BlockSpec(memory_space=pltpu.SMEM)
    return pl.pallas_call(
        hidden_kernel,
        in_specs=[smem, smem, vmem, vmem] + [anywhere] * 10,
        out_specs=vmem,
        out_shape=jax.ShapeDtypeStruct((CHIP_EXPERTS, n, ff), jnp.bfloat16),
        scratch_shapes=[
            pltpu.VMEM((CHIP_EXPERTS, n, 4 * WIDTH), jnp.bfloat16),
            pltpu.VMEM((2, 2, 4, TILES * TOK, LANES), jnp.bfloat16),
            pltpu.VMEM((2, 4 * WIDTH, 2 * ff), jnp.bfloat16),
            pltpu.SemaphoreType.DMA((2, 8 * PARTS)),
            pltpu.SemaphoreType.DMA((2, 2)),
        ],
        compiler_params=pltpu.CompilerParams(vmem_limit_bytes=48 << 20),
        cost_estimate=pl.CostEstimate(
            flops=2 * 2048 * 4096 * 1024, bytes_accessed=100 << 20, transcendentals=2048 * 384
        ),
        name="hidden",
    )(place, groups, pick, weight, *flat, *own, *far)


def down_kernel(
    part, groups, place, put, hidden, d_own, d_far, low, high, weights, y, weight_sems
):
    tiles_in = tiles_of(part)
    f, begin = len(tiles_in) * LANES, tiles_in[0][0] * LANES

    def weight_copies(e):
        return [
            pltpu.make_async_copy(
                (d_own if e < 2 else d_far).at[e % 2, :, pl.ds(x * WIDTH + begin, f)],
                weights.at[e, :, pl.ds(x * f, f)],
                weight_sems.at[e, x],
            )
            for x in range(4)
        ]

    for e in range(CHIP_EXPERTS):
        for copy in weight_copies(e):
            copy.start()
    @pl.loop(0, CHIP_EXPERTS)
    def _(e):
        for x in range(4):
            to = weights.at[e, :, pl.ds(x * f, f)]
            pltpu.make_async_copy(d_own.at[0, :, pl.ds(begin, f)], to, weight_sems.at[e, x]).wait()

        @pl.loop(0, 2)
        def _(half):
            tiles = [pl.ds(pl.multiple_of((2 * half + i) * TILE, TILE), TILE) for i in range(2)]
            used = groups[e] > 2 * half

            @pl.when(used)
            def _():
                for tile in tiles:
                    for x in range(4):
                        cols = slice(x * f, (x + 1) * f)
                        value = jnp.dot(
                            hidden[e, tile], weights[e, :, cols], preferred_element_type=jnp.float32
                        )
                        y[e, tile, cols] = value.astype(jnp.bfloat16)

            @pl.when(jnp.logical_not(used))
            def _():
                for tile in tiles:
                    y[e, tile] = jnp.zeros((TILE, 4 * f), jnp.bfloat16)

    @pl.loop(0, PAIRS, unroll=2)
    def _(pair):
        at = pl.multiple_of(pair * GROUP_ROWS, GROUP_ROWS)
        for x in range(4):
            terms = [
                y[e, pl.ds(g * TILE + at, GROUP_ROWS), x * f : (x + 1) * f]
                for e in range(CHIP_EXPERTS)
                for g in range(GROUPS)
            ]
            terms = jnp.concatenate(terms, axis=0)
            total = jnp.dot(put[pair], terms, preferred_element_type=jnp.float32)
            total = total.astype(jnp.bfloat16)
            for blk in range(2):
                piece = [
                    total[blk * TOK + start : blk * TOK + stop, i * LANES : (i + 1) * LANES]
                    for i, (_, start, stop, _) in enumerate(tiles_in)
                ]
                piece = jnp.concatenate(piece, axis=0)
                j = place[part * PEERS + (2 * pair + blk) * 4 + x]
                low[jnp.minimum(j, HALF)] = piece
                high[jnp.where(j < HALF, HALF, j - HALF)] = piece


def find_sums(part, groups, place, put, hidden, own, far):
    f, ff = len(tiles_of(part)) * LANES, own.shape[1]
    n = BLOCKS * SLOTS
    anywhere = pl.BlockSpec(memory_space=pl.ANY)
    vmem = pl.BlockSpec(memory_space=pltpu.VMEM)
    smem = pl.BlockSpec(memory_space=pltpu.SMEM)
    return pl.pallas_call(
        functools.partial(down_kernel, part),
        in_specs=[smem, smem, vmem, vmem, anywhere, anywhere],
        out_specs=[vmem] * 2,
        out_shape=[jax.ShapeDtypeStruct((HALF + 1, ROWS[part], LANES), jnp.bfloat16)] * 2,
        scratch_shapes=[
            pltpu.VMEM((CHIP_EXPERTS, ff, 4 * f), jnp.bfloat16),
            pltpu.VMEM((CHIP_EXPERTS, n, 4 * f), jnp.bfloat16),
            pltpu.SemaphoreType.DMA((CHIP_EXPERTS, 4)),
        ],
        compiler_params=pltpu.CompilerParams(vmem_limit_bytes=32 << 20),
        cost_estimate=pl.CostEstimate(
            flops=2 * 2048 * 4 * f * (ff + 256), bytes_accessed=40 << 20, transcendentals=0
        ),
        name="sums",
    )(groups, place, put, hidden, own, far)


def routing(routes, core):
    mine = jnp.where(core == 0, routes, jnp.concatenate([routes[:, 2:], routes[:, :2]], axis=1))
    marked = mine > 0
    until = jnp.asarray(np.triu(np.ones((TOK, TOK), np.float32)), jnp.bfloat16)
    rank = jnp.einsum(
        "bes,st->bet", marked.astype(jnp.bfloat16), until, preferred_element_type=jnp.float32
    )
    rank = jnp.where(marked, rank.astype(jnp.int32) - 1, -1)
    groups = jnp.max(rank, axis=(0, 2)) // SLOT_STEP + 1
    row = np.arange(GROUPS * GROUP_ROWS)
    row_slot = row // GROUP_ROWS * SLOT_STEP + row % SLOT_STEP
    row_block = row % GROUP_ROWS // SLOT_STEP
    same = jnp.asarray(row_block[:, None] == np.arange(2 * TOK)[None, :] // TOK)

    def by_pair(v):
        v = v.reshape(PAIRS, 2, CHIP_EXPERTS, TOK).transpose(0, 2, 1, 3)
        return v.reshape(PAIRS, CHIP_EXPERTS, 1, 2 * TOK)

    chosen = (by_pair(rank) == jnp.asarray(row_slot, jnp.int32)[:, None]) & same
    slot_weight = jnp.sum(jnp.where(chosen, by_pair(mine), 0.0), axis=3)
    slot_weight = slot_weight.reshape(PAIRS, CHIP_EXPERTS, GROUPS, GROUP_ROWS)
    slot_weight = slot_weight.transpose(1, 2, 0, 3).reshape(CHIP_EXPERTS, BLOCKS * SLOTS, 1)
    pick = chosen.astype(jnp.bfloat16).reshape(PAIRS, PAIR_ROWS, 2 * TOK)
    put = pick.transpose(0, 2, 1)
    return groups, pick, put, slot_weight


def spread(tokens, weights, routes):
    tiled = tokens.reshape(TOK, TILES, LANES).transpose(1, 0, 2).reshape(TILES * TOK, LANES)
    held = [tiled[None, ROW_AT[p] : ROW_AT[p] + ROWS[p]] for p in range(PARTS)]
    weights, far = list(weights), []
    for stage in range(STAGES):
        if stage != 1 and len(far) < len(weights):
            far.append(lax.ppermute(weights[len(far)], AXES, core_pairs()))
        got = [lax.ppermute(held[p], AXES, stage_pairs(p, stage)) for p in range(PARTS)]
        if stage == STAGES - 1:
            return list(zip(held, got)), far, routes
        held = [jnp.concatenate([h, g], axis=0) for h, g in zip(held, got)]
        if 1 <= stage <= 2:
            held, far, weights = lax.optimization_barrier((held, far, weights))
        if stage == 3:
            held, far, routes = lax.optimization_barrier((held, far, routes))


def add(a, b):
    return (a.astype(jnp.float32) + b.astype(jnp.float32)).astype(jnp.bfloat16)


def collect(high, low, part):
    for stage in reversed(range(STAGES)):
        got = lax.ppermute(high, AXES, stage_pairs(part, stage))
        if stage:
            cut = 1 << (stage - 1)
            high = add(low[cut : 2 * cut], got[cut : 2 * cut])
            low = add(low[:cut], got[:cut])
    return low[0].astype(jnp.float32) + got[0].astype(jnp.float32)


def on_device(
    tokens, keep_mask, expert_ids, route_weight, w_gate, w_up, w_down, norm_gain, kv_weight
):
    y, z, c, x = (lax.axis_index(a) for a in AXES)
    me = ((y * 4 + z) * 2 + c) * 4 + x
    place = lax.dynamic_index_in_dim(jnp.asarray(place_table()), me, 0, keepdims=False)

    experts = CHIP_EXPERTS * BLOCKS
    live = (keep_mask > 0)[None, None, :]
    named = expert_ids.T[None] == jnp.arange(experts, dtype=jnp.int32)[:, None, None]
    routes = jnp.sum(jnp.where(named & live, route_weight.T[None], 0.0), axis=1)
    routes = routes.reshape(BLOCKS, CHIP_EXPERTS, TOK)
    routes = lax.all_to_all(routes, ("y", "z"), split_axis=0, concat_axis=0, tiled=True)
    own = (w_gate, w_up, w_down)
    pieces, far, routes = spread(tokens, own, routes)
    groups, pick, put, slot_weight = routing(routes, c)
    hidden = find_hidden(place, groups, pick, slot_weight, pieces, own[:2], far[:2])
    totals = []
    for part in range(PARTS):
        low, high = find_sums(part, groups, place, put, hidden, own[2], far[2])
        totals.append((high, low))
    summed = jnp.concatenate([collect(*totals[p], p) for p in range(PARTS)], axis=0)
    summed = summed.reshape(TILES, TOK, LANES).transpose(1, 0, 2).reshape(TOK, WIDTH)
    mixed_out = (tokens.astype(jnp.float32) + summed).astype(jnp.bfloat16)

    full = [mixed_out] + [lax.ppermute(mixed_out, AXES, x_pairs(m)) for m in (1, 2, 3)]
    full = jnp.concatenate(full, axis=1).astype(jnp.float32)
    order = [jnp.bitwise_xor(x, m) * WIDTH for m in range(4)]
    gain = jnp.concatenate([lax.dynamic_slice_in_dim(norm_gain, o, WIDTH) for o in order])
    kv = jnp.concatenate([lax.dynamic_slice_in_dim(kv_weight, o, WIDTH) for o in order])
    mean_square = jnp.mean(full * full, axis=-1, keepdims=True)
    normed = (full * lax.rsqrt(mean_square + 1e-06) * gain).astype(jnp.bfloat16)
    kv_rows = jnp.dot(normed, kv, preferred_element_type=jnp.float32).astype(jnp.bfloat16)
    return (mixed_out, kv_rows)


def solution(mesh):
    fine = Mesh(mesh.devices.reshape(SIZES), AXES)
    ep = ("y", "z", "c")
    in_specs = (
        P(ep, "x"),
        P(ep),
        P(ep, None),
        P(ep, None),
        P(ep, None, "x"),
        P(ep, None, "x"),
        P(ep, "x", None),
        P(),
        P(None, "x"),
    )
    out_specs = (P(ep, "x"), P(ep, "x"))
    return jax.shard_map(
        on_device, mesh=fine, in_specs=in_specs, out_specs=out_specs, check_vma=False
    )
```

profile of v0, /device:TPU:0, one launch (start us, length us, event | category | flops | bytes accessed | tf_op | source)
XLA Modules:
  0.0 293.4 jit_solution(14036799251578913701)
XLA Ops:
  1.7 2.1 collective-permute-start.2
  5.3 1.6 collective-permute-start.4
  6.9 2.3 collective-permute-start.3
  9.8 3.6 %collective-permute-start.5 = (bf16[2,336,128]{2,1,0:T(8,128)(2,1)S(1)}, bf16[2,336,128]{2,1,0:T(8,128)(2,1)S(1)}, u32[]{:S(2)}, u32[]{:S(2)}) collective-permute-start(bf16[2,336,128]{2,1,0:T(8,128)(2,1)S(1)} %pad_maximum_fusion.14), channel_id=1, source_target_pairs={{0,24},{1,25},{2,26},{3,27},{4,5},{5,4},{6,7},{7,6},{8,16},{9,17},... | collective-permute-start | bytes 516104 | tf_op jit(solution)/shard_map/ppermute | solution.py:328
  13.4 3.1 %collective-permute-start.1 = (bf16[2,352,128]{2,1,0:T(8,128)(2,1)S(1)}, bf16[2,352,128]{2,1,0:T(8,128)(2,1)S(1)}, u32[]{:S(2)}, u32[]{:S(2)}) collective-permute-start(bf16[2,352,128]{2,1,0:T(8,128)(2,1)S(1)} %pad_maximum_fusion.11), channel_id=1, source_target_pairs={{0,96},{1,97},{2,98},{3,99},{4,12},{5,13},{6,14},{7,15},{8,104},{9... | collective-permute-start | bytes 540680 | tf_op jit(solution)/shard_map/ppermute | solution.py:328
  16.8 3.4 %collective-permute-done.1 = bf16[2,352,128]{2,1,0:T(8,128)(2,1)S(1)} collective-permute-done((bf16[2,352,128]{2,1,0:T(8,128)(2,1)S(1)}, bf16[2,352,128]{2,1,0:T(8,128)(2,1)S(1)}, u32[]{:S(2)}, u32[]{:S(2)}) %collective-permute-start.1) | collective-permute-done | bytes 180256 | tf_op jit(solution)/shard_map/ppermute | solution.py:328
  20.4 2.6 copy-done.9
  24.0 6.3 %collective-permute-done.8 = bf16[4,336,128]{2,1,0:T(8,128)(2,1)S(1)} collective-permute-done((bf16[4,336,128]{2,1,0:T(8,128)(2,1)S(1)}, bf16[4,336,128]{2,1,0:T(8,128)(2,1)S(1)}, u32[]{:S(2)}, u32[]{:S(2)}) %collective-permute-start.8) | collective-permute-done | bytes 344096 | tf_op jit(solution)/shard_map/ppermute | solution.py:328
  31.3 2.9 collective-permute-start.12
  34.8 2.3 collective-permute-start.11
  37.8 4.9 %all-to-all-start = ((f32[16,4,128]{2,1,0:T(4,128)}), f32[16,4,128]{2,1,0:T(4,128)}, u32[]{:S(2)}, u32[]{:S(2)}) async-start(f32[16,4,128]{2,1,0:T(4,128)} %bitcast.8), calls=%async_computation | async-start | bytes 65536 | tf_op jit(solution)/shard_map/all_to_all | solution.py:364
  44.7 2.0 collective-permute-done.13
  51.6 2.5 constant_dynamic-update-slice_fusion.3
  56.5 12.5 %collective-permute-done.17 = bf16[16,336,128]{2,1,0:T(8,128)(2,1)S(1)} collective-permute-done((bf16[16,336,128]{2,1,0:T(8,128)(2,1)}, bf16[16,336,128]{2,1,0:T(8,128)(2,1)S(1)}, u32[]{:S(2)}, u32[]{:S(2)}) %collective-permute-start.17) | collective-permute-done | bytes 1376288 | tf_op jit(solution)/shard_map/ppermute | solution.py:328
  79.5 1.9 copy.48
  81.4 1.9 and_convert_fusion
  85.2 1.9 fusion.30.put
  87.1 17.7 %collective-permute-done.18.hi1 = bf16[32,336,128]{2,1,0:T(8,128)(2,1)} collective-permute-done((bf16[32,336,128]{2,1,0:T(8,128)(2,1)}, bf16[32,336,128]{2,1,0:T(8,128)(2,1)}, u32[]{:S(2)}, u32[]{:S(2)}) %collective-permute-start.18) | collective-permute-done | bytes 2752544 | tf_op jit(solution)/shard_map/ppermute | solution.py:328
  104.7 4.8 %collective-permute-done.20.hi2 = bf16[32,336,128]{2,1,0:T(8,128)(2,1)} collective-permute-done((bf16[32,336,128]{2,1,0:T(8,128)(2,1)}, bf16[32,336,128]{2,1,0:T(8,128)(2,1)}, u32[]{:S(2)}, u32[]{:S(2)}) %collective-permute-start.20) | collective-permute-done | bytes 2752544 | tf_op jit(solution)/shard_map/ppermute | solution.py:328
  109.6 25.0 %hidden.1 = bf16[4,512,384]{2,1,0:T(8,128)(2,1)S(1)} custom-call(s32[192]{0:T(256)S(1)} %bitcast.53, s32[4]{0:T(128)S(1)} %fusion.23.groups, bf16[8,256,256]{2,1,0:T(8,128)(2,1)S(1)} %copy.53.pick, f32[4,512,1]{2,1,0:T(8,128)S(1)} %reshape.72.weight, bf16[32,352,128]{2,1,0:T(8,128)(2,1)} %constant_dynamic-update-slice_fusion.lo0, ...), custom_call_target="tpu_custom_call" | custom-call | flops 17179869184 | bytes 104857600 | tf_op jit(solution)/shard_map/hidden/pallas_call | solution.py:182
  134.5 10.7 %sums.5 = (bf16[33,336,128]{2,1,0:T(8,128)(2,1)S(1)}, bf16[33,336,128]{2,1,0:T(8,128)(2,1)}) custom-call(s32[4]{0:T(128)S(1)} %fusion.23.groups, s32[192]{0:T(256)S(1)} %bitcast.54, bf16[8,256,256]{2,1,0:T(8,128)(2,1)S(1)} %fusion.30.put, bf16[4,512,384]{2,1,0:T(8,128)(2,1)S(1)} %hidden.1, bf16[2,384,4096]{2,1,0:T(8,128)(2,1)} %d_own.5, ...), custom_call_target="tpu_custom_call" | custom-call | flops 4026531840 | bytes 41943040 | tf_op jit(solution)/shard_map/sums/pallas_call | solution.py:276
  146.3 11.1 %sums.4 = (bf16[33,336,128]{2,1,0:T(8,128)(2,1)S(1)}, bf16[33,336,128]{2,1,0:T(8,128)(2,1)}) custom-call(s32[4]{0:T(128)S(1)} %fusion.23.groups, s32[192]{0:T(256)S(1)} %bitcast.55, bf16[8,256,256]{2,1,0:T(8,128)(2,1)S(1)} %fusion.30.put, bf16[4,512,384]{2,1,0:T(8,128)(2,1)S(1)} %hidden.1, bf16[2,384,4096]{2,1,0:T(8,128)(2,1)} %d_own.5, ...), custom_call_target="tpu_custom_call" | custom-call | flops 5368709120 | bytes 41943040 | tf_op jit(solution)/shard_map/sums/pallas_call | solution.py:276
  157.5 2.3 collective-permute-start.27
  159.7 9.0 %sums.3 = (bf16[33,352,128]{2,1,0:T(8,128)(2,1)S(1)}, bf16[33,352,128]{2,1,0:T(8,128)(2,1)S(1)}) custom-call(s32[4]{0:T(128)S(1)} %fusion.23.groups, s32[192]{0:T(256)S(1)} %bitcast.56, bf16[8,256,256]{2,1,0:T(8,128)(2,1)S(1)} %fusion.30.put, bf16[4,512,384]{2,1,0:T(8,128)(2,1)S(1)} %hidden.1, bf16[2,384,4096]{2,1,0:T(8,128)(2,1)} %d_own.5, ...), custom_call_target="tpu_custom_call" | custom-call | flops 4026531840 | bytes 41943040 | tf_op jit(solution)/shard_map/sums/pallas_call | solution.py:276
  168.8 2.2 collective-permute-start.21
  171.0 9.8 %collective-permute-done.33 = bf16[33,336,128]{2,1,0:T(8,128)(2,1)} collective-permute-done((bf16[33,336,128]{2,1,0:T(8,128)(2,1)}, bf16[33,336,128]{2,1,0:T(8,128)(2,1)}, u32[]{:S(2)}, u32[]{:S(2)}) %collective-permute-start.33) | collective-permute-done | bytes 2838560 | tf_op jit(solution)/shard_map/ppermute | solution.py:344
  180.8 2.5 add_convert_fusion.3
  183.3 1.8 collective-permute-start.34
  185.1 7.9 %collective-permute-done.27 = bf16[33,336,128]{2,1,0:T(8,128)(2,1)} collective-permute-done((bf16[33,336,128]{2,1,0:T(8,128)(2,1)}, bf16[33,336,128]{2,1,0:T(8,128)(2,1)}, u32[]{:S(2)}, u32[]{:S(2)}) %collective-permute-start.27) | collective-permute-done | bytes 2838560 | tf_op jit(solution)/shard_map/ppermute | solution.py:344
  193.0 2.5 add_convert_fusion.5
  195.6 9.9 %collective-permute-done.21 = bf16[33,352,128]{2,1,0:T(8,128)(2,1)S(1)} collective-permute-done((bf16[33,352,128]{2,1,0:T(8,128)(2,1)S(1)}, bf16[33,352,128]{2,1,0:T(8,128)(2,1)S(1)}, u32[]{:S(2)}, u32[]{:S(2)}) %collective-permute-start.21) | collective-permute-done | bytes 2973728 | tf_op jit(solution)/shard_map/ppermute | solution.py:344
  206.2 4.3 %collective-permute-start.22 = (bf16[16,352,128]{2,1,0:T(8,128)(2,1)S(1)}, bf16[16,352,128]{2,1,0:T(8,128)(2,1)S(1)}, u32[]{:S(2)}, u32[]{:S(2)}) collective-permute-start(bf16[16,352,128]{2,1,0:T(8,128)(2,1)S(1)} %get-tuple-element.53), channel_id=1, source_target_pairs={{0,32},{1,33},{2,34},{3,35},{4,28},{5,29},{6,30},{7,31},{8,40},{9,... | collective-permute-start | bytes 4325384 | tf_op jit(solution)/shard_map/ppermute | solution.py:344
  211.8 3.4 %collective-permute-start.35 = (bf16[8,336,128]{2,1,0:T(8,128)(2,1)}, bf16[8,336,128]{2,1,0:T(8,128)(2,1)}, u32[]{:S(2)}, u32[]{:S(2)}) collective-permute-start(bf16[8,336,128]{2,1,0:T(8,128)(2,1)} %get-tuple-element.63), channel_id=1, source_target_pairs={{0,96},{1,97},{2,98},{3,99},{4,12},{5,13},{6,14},{7,15},{8,104},{9... | collective-permute-start | bytes 2064392 | tf_op jit(solution)/shard_map/ppermute | solution.py:344
  216.5 8.8 %collective-permute-start.29 = (bf16[8,336,128]{2,1,0:T(8,128)(2,1)}, bf16[8,336,128]{2,1,0:T(8,128)(2,1)}, u32[]{:S(2)}, u32[]{:S(2)}) collective-permute-start(bf16[8,336,128]{2,1,0:T(8,128)(2,1)} %get-tuple-element.61), channel_id=1, source_target_pairs={{0,24},{1,25},{2,26},{3,27},{4,5},{5,4},{6,7},{7,6},{8,16},{9,17},... | collective-permute-start | bytes 2064392 | tf_op jit(solution)/shard_map/ppermute | solution.py:344
  225.3 6.2 %collective-permute-done.22 = bf16[16,352,128]{2,1,0:T(8,128)(2,1)S(1)} collective-permute-done((bf16[16,352,128]{2,1,0:T(8,128)(2,1)S(1)}, bf16[16,352,128]{2,1,0:T(8,128)(2,1)S(1)}, u32[]{:S(2)}, u32[]{:S(2)}) %collective-permute-start.22) | collective-permute-done | bytes 1441824 | tf_op jit(solution)/shard_map/ppermute | solution.py:344
  231.9 2.6 collective-permute-start.23
  235.8 2.4 collective-permute-done.29
  239.5 2.6 collective-permute-start.30
  242.0 6.3 %collective-permute-done.23 = bf16[8,352,128]{2,1,0:T(8,128)(2,1)S(1)} collective-permute-done((bf16[8,352,128]{2,1,0:T(8,128)(2,1)S(1)}, bf16[8,352,128]{2,1,0:T(8,128)(2,1)S(1)}, u32[]{:S(2)}, u32[]{:S(2)}) %collective-permute-start.23) | collective-permute-done | bytes 720928 | tf_op jit(solution)/shard_map/ppermute | solution.py:344
  248.7 5.5 %collective-permute-start.37 = (bf16[2,336,128]{2,1,0:T(8,128)(2,1)S(1)}, bf16[2,336,128]{2,1,0:T(8,128)(2,1)S(1)}, u32[]{:S(2)}, u32[]{:S(2)}) collective-permute-start(bf16[2,336,128]{2,1,0:T(8,128)(2,1)S(1)} %get-tuple-element.79), channel_id=1, source_target_pairs={{0,24},{1,25},{2,26},{3,27},{4,5},{5,4},{6,7},{7,6},{8,16},{9,17},... | collective-permute-start | bytes 516104 | tf_op jit(solution)/shard_map/ppermute | solution.py:344
  254.3 2.4 collective-permute-start.31
  257.6 2.5 collective-permute-start.38
  262.6 9.7 %collective-permute-start.25 = (bf16[2,352,128]{2,1,0:T(8,128)(2,1)S(1)}, bf16[2,352,128]{2,1,0:T(8,128)(2,1)S(1)}, u32[]{:S(2)}, u32[]{:S(2)}) collective-permute-start(bf16[2,352,128]{2,1,0:T(8,128)(2,1)S(1)} %get-tuple-element.75), channel_id=1, source_target_pairs={{0,96},{1,97},{2,98},{3,99},{4,12},{5,13},{6,14},{7,15},{8,104},{9... | collective-permute-start | bytes 540680 | tf_op jit(solution)/shard_map/ppermute | solution.py:344
  272.4 3.4 %collective-permute-done.25 = bf16[2,352,128]{2,1,0:T(8,128)(2,1)S(1)} collective-permute-done((bf16[2,352,128]{2,1,0:T(8,128)(2,1)S(1)}, bf16[2,352,128]{2,1,0:T(8,128)(2,1)S(1)}, u32[]{:S(2)}, u32[]{:S(2)}) %collective-permute-start.25) | collective-permute-done | bytes 180256 | tf_op jit(solution)/shard_map/ppermute | solution.py:344
  276.0 4.5 %collective-permute-done.26 = bf16[1,352,128]{2,1,0:T(8,128)(2,1)S(1)} collective-permute-done((bf16[1,352,128]{2,1,0:T(8,128)(2,1)S(1)}, bf16[1,352,128]{2,1,0:T(8,128)(2,1)S(1)}, u32[]{:S(2)}, u32[]{:S(2)}) %collective-permute-start.26) | collective-permute-done | bytes 90144 | tf_op jit(solution)/shard_map/ppermute | solution.py:344
  280.6 2.5 collective-permute-start.41
  283.1 1.6 collective-permute-start.39
  284.9 4.9 %collective-permute-done.41 = bf16[128,1024]{1,0:T(8,128)(2,1)S(1)} collective-permute-done((bf16[128,1024]{1,0:T(8,128)(2,1)S(1)}, bf16[128,1024]{1,0:T(8,128)(2,1)S(1)}, u32[]{:S(2)}, u32[]{:S(2)}) %collective-permute-start.41) | collective-permute-done | bytes 262176 | tf_op jit(solution)/shard_map/ppermute | solution.py:377
  (140 shorter events, 43.7 us)
Async XLA Ops:
  0.6 19.7 %collective-permute-start.6 = (bf16[2,4096,384]{2,1,0:T(8,128)(2,1)}, bf16[2,4096,384]{2,1,0:T(8,128)(2,1)S(1)}, u32[]{:S(2)}, u32[]{:S(2)}) collective-permute-start(bf16[2,4096,384]{2,1,0:T(8,128)(2,1)} %g_own.1), channel_id=1, source_target_pairs={{0,4},{1,5},{2,6},{3,7},{4,0},{5,1},{6,2},{7,3},{8,12},{9,13},{10,... | collective-permute-start | bytes 18874376 | tf_op jit(solution)/shard_map/ppermute | solution.py:327
  1.7 5.2 %collective-permute-start.2 = (bf16[1,336,128]{2,1,0:T(8,128)(2,1)S(1)}, bf16[1,336,128]{2,1,0:T(8,128)(2,1)S(1)}, u32[]{:S(2)}, u32[]{:S(2)}) collective-permute-start(bf16[1,336,128]{2,1,0:T(8,128)(2,1)S(1)} %get-tuple-element.81), channel_id=1, source_target_pairs={{0,8},{1,9},{2,10},{3,11},{4,7},{5,6},{6,5},{7,4},{8,0},{9,1},{10,... | collective-permute-start | bytes 258056 | tf_op jit(solution)/shard_map/ppermute | solution.py:328
  3.8 9.6 %collective-permute-start = (bf16[1,352,128]{2,1,0:T(8,128)(2,1)S(1)}, bf16[1,352,128]{2,1,0:T(8,128)(2,1)S(1)}, u32[]{:S(2)}, u32[]{:S(2)}) collective-permute-start(bf16[1,352,128]{2,1,0:T(8,128)(2,1)S(1)} %slice_bitcast_fusion), channel_id=1, source_target_pairs={{0,1},{1,0},{2,3},{3,2},{4,100},{5,101},{6,102},{7,103},{8,9},{9,8... | collective-permute-start | bytes 270344 | tf_op jit(solution)/shard_map/ppermute | solution.py:328
  5.3 4.5 %collective-permute-start.4 = (bf16[1,336,128]{2,1,0:T(8,128)(2,1)S(1)}, bf16[1,336,128]{2,1,0:T(8,128)(2,1)S(1)}, u32[]{:S(2)}, u32[]{:S(2)}) collective-permute-start(bf16[1,336,128]{2,1,0:T(8,128)(2,1)S(1)} %get-tuple-element.80), channel_id=1, source_target_pairs={{0,32},{1,33},{2,34},{3,35},{4,28},{5,29},{6,30},{7,31},{8,40},{9,... | collective-permute-start | bytes 258056 | tf_op jit(solution)/shard_map/ppermute | solution.py:328
  6.9 9.6 %collective-permute-start.3 = (bf16[2,336,128]{2,1,0:T(8,128)(2,1)S(1)}, bf16[2,336,128]{2,1,0:T(8,128)(2,1)S(1)}, u32[]{:S(2)}, u32[]{:S(2)}) collective-permute-start(bf16[2,336,128]{2,1,0:T(8,128)(2,1)S(1)} %pad_maximum_fusion.13), channel_id=1, source_target_pairs={{0,3},{1,2},{2,1},{3,0},{4,36},{5,37},{6,38},{7,39},{8,11},{9,10},... | collective-permute-start | bytes 516104 | tf_op jit(solution)/shard_map/ppermute | solution.py:328
  9.8 7.0 %collective-permute-start.5 = (bf16[2,336,128]{2,1,0:T(8,128)(2,1)S(1)}, bf16[2,336,128]{2,1,0:T(8,128)(2,1)S(1)}, u32[]{:S(2)}, u32[]{:S(2)}) collective-permute-start(bf16[2,336,128]{2,1,0:T(8,128)(2,1)S(1)} %pad_maximum_fusion.14), channel_id=1, source_target_pairs={{0,24},{1,25},{2,26},{3,27},{4,5},{5,4},{6,7},{7,6},{8,16},{9,17},... | collective-permute-start | bytes 516104 | tf_op jit(solution)/shard_map/ppermute | solution.py:328
  13.4 6.8 %collective-permute-start.1 = (bf16[2,352,128]{2,1,0:T(8,128)(2,1)S(1)}, bf16[2,352,128]{2,1,0:T(8,128)(2,1)S(1)}, u32[]{:S(2)}, u32[]{:S(2)}) collective-permute-start(bf16[2,352,128]{2,1,0:T(8,128)(2,1)S(1)} %pad_maximum_fusion.11), channel_id=1, source_target_pairs={{0,96},{1,97},{2,98},{3,99},{4,12},{5,13},{6,14},{7,15},{8,104},{9... | collective-permute-start | bytes 540680 | tf_op jit(solution)/shard_map/ppermute | solution.py:328
  20.3 16.8 %copy-start.11 = (s32[128]{0:T(128)S(1)}, s32[128]{0:T(128)}, u32[]{:S(2)}) copy-start(s32[128]{0:T(128)} %param.14) | copy-start | bytes 1540
  20.3 16.8 %copy-start.6 = (f32[128,8]{0,1:T(8,128)S(1)}, f32[128,8]{0,1:T(8,128)}, u32[]{:S(2)}) copy-start(f32[128,8]{0,1:T(8,128)} %param.16) | copy-start | bytes 12292
  20.3 16.8 %copy-start.7 = (s32[128,8]{0,1:T(8,128)S(1)}, s32[128,8]{0,1:T(8,128)}, u32[]{:S(2)}) copy-start(s32[128,8]{0,1:T(8,128)} %param.15) | copy-start | bytes 12292
  20.3 10.8 %collective-permute-start.10 = (bf16[2,4096,384]{2,1,0:T(8,128)(2,1)}, bf16[2,4096,384]{2,1,0:T(8,128)(2,1)S(1)}, u32[]{:S(2)}, u32[]{:S(2)}) collective-permute-start(bf16[2,4096,384]{2,1,0:T(8,128)(2,1)} %u_own.1), channel_id=1, source_target_pairs={{0,4},{1,5},{2,6},{3,7},{4,0},{5,1},{6,2},{7,3},{8,12},{9,13},{10,... | collective-permute-start | bytes 18874376 | tf_op jit(solution)/shard_map/ppermute | solution.py:327
  23.0 7.2 %collective-permute-start.8 = (bf16[4,336,128]{2,1,0:T(8,128)(2,1)S(1)}, bf16[4,336,128]{2,1,0:T(8,128)(2,1)S(1)}, u32[]{:S(2)}, u32[]{:S(2)}) collective-permute-start(bf16[4,336,128]{2,1,0:T(8,128)(2,1)S(1)} %pad_maximum_fusion.9), channel_id=1, source_target_pairs={{0,32},{1,33},{2,34},{3,35},{4,28},{5,29},{6,30},{7,31},{8,40},{9,... | collective-permute-start | bytes 1032200 | tf_op jit(solution)/shard_map/ppermute | solution.py:328
  23.4 7.2 %collective-permute-start.9 = (bf16[4,336,128]{2,1,0:T(8,128)(2,1)S(1)}, bf16[4,336,128]{2,1,0:T(8,128)(2,1)S(1)}, u32[]{:S(2)}, u32[]{:S(2)}) collective-permute-start(bf16[4,336,128]{2,1,0:T(8,128)(2,1)S(1)} %pad_maximum_fusion.10), channel_id=1, source_target_pairs={{0,1},{1,0},{2,3},{3,2},{4,100},{5,101},{6,102},{7,103},{8,9},{9,8... | collective-permute-start | bytes 1032200 | tf_op jit(solution)/shard_map/ppermute | solution.py:328
  23.6 7.4 %collective-permute-start.7 = (bf16[4,352,128]{2,1,0:T(8,128)(2,1)S(1)}, bf16[4,352,128]{2,1,0:T(8,128)(2,1)S(1)}, u32[]{:S(2)}, u32[]{:S(2)}) collective-permute-start(bf16[4,352,128]{2,1,0:T(8,128)(2,1)S(1)} %pad_maximum_fusion.8), channel_id=1, source_target_pairs={{0,8},{1,9},{2,10},{3,11},{4,7},{5,6},{6,5},{7,4},{8,0},{9,1},{10,... | collective-permute-start | bytes 1081352 | tf_op jit(solution)/shard_map/ppermute | solution.py:328
  31.1 19.4 %collective-permute-start.14 = (bf16[2,384,4096]{2,1,0:T(8,128)(2,1)}, bf16[2,384,4096]{2,1,0:T(8,128)(2,1)}, u32[]{:S(2)}, u32[]{:S(2)}) collective-permute-start(bf16[2,384,4096]{2,1,0:T(8,128)(2,1)} %d_own.5), channel_id=1, source_target_pairs={{0,4},{1,5},{2,6},{3,7},{4,0},{5,1},{6,2},{7,3},{8,12},{9,13},{10,... | collective-permute-start | bytes 18874376 | tf_op jit(solution)/shard_map/ppermute | solution.py:327
  31.3 12.1 %collective-permute-start.12 = (bf16[8,336,128]{2,1,0:T(8,128)(2,1)S(1)}, bf16[8,336,128]{2,1,0:T(8,128)(2,1)S(1)}, u32[]{:S(2)}, u32[]{:S(2)}) collective-permute-start(bf16[8,336,128]{2,1,0:T(8,128)(2,1)S(1)} %pad_maximum_fusion.5), channel_id=1, source_target_pairs={{0,24},{1,25},{2,26},{3,27},{4,5},{5,4},{6,7},{7,6},{8,16},{9,17},... | collective-permute-start | bytes 2064392 | tf_op jit(solution)/shard_map/ppermute | solution.py:328
  34.2 12.4 %collective-permute-start.13 = (bf16[8,336,128]{2,1,0:T(8,128)(2,1)S(1)}, bf16[8,336,128]{2,1,0:T(8,128)(2,1)}, u32[]{:S(2)}, u32[]{:S(2)}) collective-permute-start(bf16[8,336,128]{2,1,0:T(8,128)(2,1)S(1)} %pad_maximum_fusion.6), channel_id=1, source_target_pairs={{0,96},{1,97},{2,98},{3,99},{4,12},{5,13},{6,14},{7,15},{8,104},{9... | collective-permute-start | bytes 2064392 | tf_op jit(solution)/shard_map/ppermute | solution.py:328
  34.8 13.1 %collective-permute-start.11 = (bf16[8,352,128]{2,1,0:T(8,128)(2,1)S(1)}, bf16[8,352,128]{2,1,0:T(8,128)(2,1)}, u32[]{:S(2)}, u32[]{:S(2)}) collective-permute-start(bf16[8,352,128]{2,1,0:T(8,128)(2,1)S(1)} %pad_maximum_fusion.4), channel_id=1, source_target_pairs={{0,3},{1,2},{2,1},{3,0},{4,36},{5,37},{6,38},{7,39},{8,11},{9,10},... | collective-permute-start | bytes 2162696 | tf_op jit(solution)/shard_map/ppermute | solution.py:328
  37.8 12.6 %all-to-all-start = ((f32[16,4,128]{2,1,0:T(4,128)}), f32[16,4,128]{2,1,0:T(4,128)}, u32[]{:S(2)}, u32[]{:S(2)}) async-start(f32[16,4,128]{2,1,0:T(4,128)} %bitcast.8), calls=%async_computation | async-start | bytes 65536 | tf_op jit(solution)/shard_map/all_to_all | solution.py:364
  50.5 18.5 %collective-permute-start.17 = (bf16[16,336,128]{2,1,0:T(8,128)(2,1)}, bf16[16,336,128]{2,1,0:T(8,128)(2,1)S(1)}, u32[]{:S(2)}, u32[]{:S(2)}) collective-permute-start(bf16[16,336,128]{2,1,0:T(8,128)(2,1)} %pad_maximum_fusion.1), channel_id=1, source_target_pairs={{0,1},{1,0},{2,3},{3,2},{4,100},{5,101},{6,102},{7,103},{8,9},{9,8... | collective-permute-start | bytes 4128776 | tf_op jit(solution)/shard_map/ppermute | solution.py:328
  50.5 20.7 %collective-permute-start.15 = (bf16[16,352,128]{2,1,0:T(8,128)(2,1)S(1)}, bf16[16,352,128]{2,1,0:T(8,128)(2,1)S(1)}, u32[]{:S(2)}, u32[]{:S(2)}) collective-permute-start(bf16[16,352,128]{2,1,0:T(8,128)(2,1)S(1)} %pad_maximum_fusion), channel_id=1, source_target_pairs={{0,32},{1,33},{2,34},{3,35},{4,28},{5,29},{6,30},{7,31},{8,40},{9,... | collective-permute-start | bytes 4325384 | tf_op jit(solution)/shard_map/ppermute | solution.py:328
  51.0 22.8 %collective-permute-start.19 = (bf16[16,336,128]{2,1,0:T(8,128)(2,1)S(1)}, bf16[16,336,128]{2,1,0:T(8,128)(2,1)S(1)}, u32[]{:S(2)}, u32[]{:S(2)}) collective-permute-start(bf16[16,336,128]{2,1,0:T(8,128)(2,1)S(1)} %pad_maximum_fusion.2), channel_id=1, source_target_pairs={{0,8},{1,9},{2,10},{3,11},{4,7},{5,6},{6,5},{7,4},{8,0},{9,1},{10,... | collective-permute-start | bytes 4128776 | tf_op jit(solution)/shard_map/ppermute | solution.py:328
  70.2 34.6 %collective-permute-start.18 = (bf16[32,336,128]{2,1,0:T(8,128)(2,1)}, bf16[32,336,128]{2,1,0:T(8,128)(2,1)}, u32[]{:S(2)}, u32[]{:S(2)}) collective-permute-start(bf16[32,336,128]{2,1,0:T(8,128)(2,1)} %constant_dynamic-update-slice_fusion.2.lo1), channel_id=1, source_target_pairs={{0,96},{1,97},{2,98},{3,99},{4,12},{5,13},{6,14},{7,15},{8,104},{9... | collective-permute-start | bytes 8257544 | tf_op jit(solution)/shard_map/ppermute | solution.py:328
  72.5 37.1 %collective-permute-start.16 = (bf16[32,352,128]{2,1,0:T(8,128)(2,1)}, bf16[32,352,128]{2,1,0:T(8,128)(2,1)}, u32[]{:S(2)}, u32[]{:S(2)}) collective-permute-start(bf16[32,352,128]{2,1,0:T(8,128)(2,1)} %constant_dynamic-update-slice_fusion.lo0), channel_id=1, source_target_pairs={{0,24},{1,25},{2,26},{3,27},{4,5},{5,4},{6,7},{7,6},{8,16},{9,17},... | collective-permute-start | bytes 8650760 | tf_op jit(solution)/shard_map/ppermute | solution.py:328
  75.0 34.6 %collective-permute-start.20 = (bf16[32,336,128]{2,1,0:T(8,128)(2,1)}, bf16[32,336,128]{2,1,0:T(8,128)(2,1)}, u32[]{:S(2)}, u32[]{:S(2)}) collective-permute-start(bf16[32,336,128]{2,1,0:T(8,128)(2,1)} %constant_dynamic-update-slice_fusion.4.lo2), channel_id=1, source_target_pairs={{0,3},{1,2},{2,1},{3,0},{4,36},{5,37},{6,38},{7,39},{8,11},{9,10},... | collective-permute-start | bytes 8257544 | tf_op jit(solution)/shard_map/ppermute | solution.py:328
  145.2 35.6 %collective-permute-start.33 = (bf16[33,336,128]{2,1,0:T(8,128)(2,1)}, bf16[33,336,128]{2,1,0:T(8,128)(2,1)}, u32[]{:S(2)}, u32[]{:S(2)}) collective-permute-start(bf16[33,336,128]{2,1,0:T(8,128)(2,1)} %get-tuple-element.51), channel_id=1, source_target_pairs={{0,3},{1,2},{2,1},{3,0},{4,36},{5,37},{6,38},{7,39},{8,11},{9,10},... | collective-permute-start | bytes 8515592 | tf_op jit(solution)/shard_map/ppermute | solution.py:344
  157.5 35.6 %collective-permute-start.27 = (bf16[33,336,128]{2,1,0:T(8,128)(2,1)}, bf16[33,336,128]{2,1,0:T(8,128)(2,1)}, u32[]{:S(2)}, u32[]{:S(2)}) collective-permute-start(bf16[33,336,128]{2,1,0:T(8,128)(2,1)} %get-tuple-element.49), channel_id=1, source_target_pairs={{0,96},{1,97},{2,98},{3,99},{4,12},{5,13},{6,14},{7,15},{8,104},{9... | collective-permute-start | bytes 8515592 | tf_op jit(solution)/shard_map/ppermute | solution.py:344
  168.8 36.7 %collective-permute-start.21 = (bf16[33,352,128]{2,1,0:T(8,128)(2,1)S(1)}, bf16[33,352,128]{2,1,0:T(8,128)(2,1)S(1)}, u32[]{:S(2)}, u32[]{:S(2)}) collective-permute-start(bf16[33,352,128]{2,1,0:T(8,128)(2,1)S(1)} %get-tuple-element.47), channel_id=1, source_target_pairs={{0,24},{1,25},{2,26},{3,27},{4,5},{5,4},{6,7},{7,6},{8,16},{9,17},... | collective-permute-start | bytes 8921096 | tf_op jit(solution)/shard_map/ppermute | solution.py:344
  183.3 27.2 %collective-permute-start.34 = (bf16[16,336,128]{2,1,0:T(8,128)(2,1)S(1)}, bf16[16,336,128]{2,1,0:T(8,128)(2,1)S(1)}, u32[]{:S(2)}, u32[]{:S(2)}) collective-permute-start(bf16[16,336,128]{2,1,0:T(8,128)(2,1)S(1)} %get-tuple-element.57), channel_id=1, source_target_pairs={{0,8},{1,9},{2,10},{3,11},{4,7},{5,6},{6,5},{7,4},{8,0},{9,1},{10,... | collective-permute-start | bytes 4128776 | tf_op jit(solution)/shard_map/ppermute | solution.py:344
  195.5 19.7 %collective-permute-start.28 = (bf16[16,336,128]{2,1,0:T(8,128)(2,1)S(1)}, bf16[16,336,128]{2,1,0:T(8,128)(2,1)S(1)}, u32[]{:S(2)}, u32[]{:S(2)}) collective-permute-start(bf16[16,336,128]{2,1,0:T(8,128)(2,1)S(1)} %get-tuple-element.55), channel_id=1, source_target_pairs={{0,1},{1,0},{2,3},{3,2},{4,100},{5,101},{6,102},{7,103},{8,9},{9,8... | collective-permute-start | bytes 4128776 | tf_op jit(solution)/shard_map/ppermute | solution.py:344
  206.2 25.3 %collective-permute-start.22 = (bf16[16,352,128]{2,1,0:T(8,128)(2,1)S(1)}, bf16[16,352,128]{2,1,0:T(8,128)(2,1)S(1)}, u32[]{:S(2)}, u32[]{:S(2)}) collective-permute-start(bf16[16,352,128]{2,1,0:T(8,128)(2,1)S(1)} %get-tuple-element.53), channel_id=1, source_target_pairs={{0,32},{1,33},{2,34},{3,35},{4,28},{5,29},{6,30},{7,31},{8,40},{9,... | collective-permute-start | bytes 4325384 | tf_op jit(solution)/shard_map/ppermute | solution.py:344
  211.8 22.7 %collective-permute-start.35 = (bf16[8,336,128]{2,1,0:T(8,128)(2,1)}, bf16[8,336,128]{2,1,0:T(8,128)(2,1)}, u32[]{:S(2)}, u32[]{:S(2)}) collective-permute-start(bf16[8,336,128]{2,1,0:T(8,128)(2,1)} %get-tuple-element.63), channel_id=1, source_target_pairs={{0,96},{1,97},{2,98},{3,99},{4,12},{5,13},{6,14},{7,15},{8,104},{9... | collective-permute-start | bytes 2064392 | tf_op jit(solution)/shard_map/ppermute | solution.py:344
  216.5 21.7 %collective-permute-start.29 = (bf16[8,336,128]{2,1,0:T(8,128)(2,1)}, bf16[8,336,128]{2,1,0:T(8,128)(2,1)}, u32[]{:S(2)}, u32[]{:S(2)}) collective-permute-start(bf16[8,336,128]{2,1,0:T(8,128)(2,1)} %get-tuple-element.61), channel_id=1, source_target_pairs={{0,24},{1,25},{2,26},{3,27},{4,5},{5,4},{6,7},{7,6},{8,16},{9,17},... | collective-permute-start | bytes 2064392 | tf_op jit(solution)/shard_map/ppermute | solution.py:344
  231.9 16.4 %collective-permute-start.23 = (bf16[8,352,128]{2,1,0:T(8,128)(2,1)S(1)}, bf16[8,352,128]{2,1,0:T(8,128)(2,1)S(1)}, u32[]{:S(2)}, u32[]{:S(2)}) collective-permute-start(bf16[8,352,128]{2,1,0:T(8,128)(2,1)S(1)} %get-tuple-element.59), channel_id=1, source_target_pairs={{0,3},{1,2},{2,1},{3,0},{4,36},{5,37},{6,38},{7,39},{8,11},{9,10},... | collective-permute-start | bytes 2162696 | tf_op jit(solution)/shard_map/ppermute | solution.py:344
  235.8 12.9 %collective-permute-start.36 = (bf16[4,336,128]{2,1,0:T(8,128)(2,1)S(1)}, bf16[4,336,128]{2,1,0:T(8,128)(2,1)S(1)}, u32[]{:S(2)}, u32[]{:S(2)}) collective-permute-start(bf16[4,336,128]{2,1,0:T(8,128)(2,1)S(1)} %get-tuple-element.73), channel_id=1, source_target_pairs={{0,1},{1,0},{2,3},{3,2},{4,100},{5,101},{6,102},{7,103},{8,9},{9,8... | collective-permute-start | bytes 1032200 | tf_op jit(solution)/shard_map/ppermute | solution.py:344
  239.5 14.8 %collective-permute-start.30 = (bf16[4,336,128]{2,1,0:T(8,128)(2,1)S(1)}, bf16[4,336,128]{2,1,0:T(8,128)(2,1)S(1)}, u32[]{:S(2)}, u32[]{:S(2)}) collective-permute-start(bf16[4,336,128]{2,1,0:T(8,128)(2,1)S(1)} %get-tuple-element.71), channel_id=1, source_target_pairs={{0,32},{1,33},{2,34},{3,35},{4,28},{5,29},{6,30},{7,31},{8,40},{9,... | collective-permute-start | bytes 1032200 | tf_op jit(solution)/shard_map/ppermute | solution.py:344
  248.5 14.0 %collective-permute-start.24 = (bf16[4,352,128]{2,1,0:T(8,128)(2,1)S(1)}, bf16[4,352,128]{2,1,0:T(8,128)(2,1)S(1)}, u32[]{:S(2)}, u32[]{:S(2)}) collective-permute-start(bf16[4,352,128]{2,1,0:T(8,128)(2,1)S(1)} %get-tuple-element.69), channel_id=1, source_target_pairs={{0,8},{1,9},{2,10},{3,11},{4,7},{5,6},{6,5},{7,4},{8,0},{9,1},{10,... | collective-permute-start | bytes 1081352 | tf_op jit(solution)/shard_map/ppermute | solution.py:344
  248.7 8.9 %collective-permute-start.37 = (bf16[2,336,128]{2,1,0:T(8,128)(2,1)S(1)}, bf16[2,336,128]{2,1,0:T(8,128)(2,1)S(1)}, u32[]{:S(2)}, u32[]{:S(2)}) collective-permute-start(bf16[2,336,128]{2,1,0:T(8,128)(2,1)S(1)} %get-tuple-element.79), channel_id=1, source_target_pairs={{0,24},{1,25},{2,26},{3,27},{4,5},{5,4},{6,7},{7,6},{8,16},{9,17},... | collective-permute-start | bytes 516104 | tf_op jit(solution)/shard_map/ppermute | solution.py:344
  254.3 6.7 %collective-permute-start.31 = (bf16[2,336,128]{2,1,0:T(8,128)(2,1)S(1)}, bf16[2,336,128]{2,1,0:T(8,128)(2,1)S(1)}, u32[]{:S(2)}, u32[]{:S(2)}) collective-permute-start(bf16[2,336,128]{2,1,0:T(8,128)(2,1)S(1)} %get-tuple-element.77), channel_id=1, source_target_pairs={{0,3},{1,2},{2,1},{3,0},{4,36},{5,37},{6,38},{7,39},{8,11},{9,10},... | collective-permute-start | bytes 516104 | tf_op jit(solution)/shard_map/ppermute | solution.py:344
  257.6 22.9 %copy-start.1 = (bf16[128,1024]{1,0:T(8,128)(2,1)S(1)}, bf16[128,1024]{1,0:T(8,128)(2,1)}, u32[]{:S(2)}) copy-start(bf16[128,1024]{1,0:T(8,128)(2,1)} %param.13) | copy-start | bytes 786436
  257.6 14.7 %collective-permute-start.38 = (bf16[1,336,128]{2,1,0:T(8,128)(2,1)S(1)}, bf16[1,336,128]{2,1,0:T(8,128)(2,1)S(1)}, u32[]{:S(2)}, u32[]{:S(2)}) collective-permute-start(bf16[1,336,128]{2,1,0:T(8,128)(2,1)S(1)} %add_convert_fusion.26), channel_id=1, source_target_pairs={{0,32},{1,33},{2,34},{3,35},{4,28},{5,29},{6,30},{7,31},{8,40},{9,... | collective-permute-start | bytes 258056 | tf_op jit(solution)/shard_map/ppermute | solution.py:344
  261.1 14.9 %collective-permute-start.32 = (bf16[1,336,128]{2,1,0:T(8,128)(2,1)S(1)}, bf16[1,336,128]{2,1,0:T(8,128)(2,1)S(1)}, u32[]{:S(2)}, u32[]{:S(2)}) collective-permute-start(bf16[1,336,128]{2,1,0:T(8,128)(2,1)S(1)} %add_convert_fusion.28), channel_id=1, source_target_pairs={{0,8},{1,9},{2,10},{3,11},{4,7},{5,6},{6,5},{7,4},{8,0},{9,1},{10,... | collective-permute-start | bytes 258056 | tf_op jit(solution)/shard_map/ppermute | solution.py:344
  262.6 22.1 %copy-start = (bf16[4096,256]{1,0:T(8,128)(2,1)S(1)}, bf16[4096,256]{1,0:T(8,128)(2,1)}, u32[]{:S(2)}) copy-start(bf16[4096,256]{1,0:T(8,128)(2,1)} %param.21) | copy-start | bytes 6291460
  262.6 13.1 %collective-permute-start.25 = (bf16[2,352,128]{2,1,0:T(8,128)(2,1)S(1)}, bf16[2,352,128]{2,1,0:T(8,128)(2,1)S(1)}, u32[]{:S(2)}, u32[]{:S(2)}) collective-permute-start(bf16[2,352,128]{2,1,0:T(8,128)(2,1)S(1)} %get-tuple-element.75), channel_id=1, source_target_pairs={{0,96},{1,97},{2,98},{3,99},{4,12},{5,13},{6,14},{7,15},{8,104},{9... | collective-permute-start | bytes 540680 | tf_op jit(solution)/shard_map/ppermute | solution.py:344
  275.8 4.6 %collective-permute-start.26 = (bf16[1,352,128]{2,1,0:T(8,128)(2,1)S(1)}, bf16[1,352,128]{2,1,0:T(8,128)(2,1)S(1)}, u32[]{:S(2)}, u32[]{:S(2)}) collective-permute-start(bf16[1,352,128]{2,1,0:T(8,128)(2,1)S(1)} %add_convert_fusion.24), channel_id=1, source_target_pairs={{0,1},{1,0},{2,3},{3,2},{4,100},{5,101},{6,102},{7,103},{8,9},{9,8... | collective-permute-start | bytes 270344 | tf_op jit(solution)/shard_map/ppermute | solution.py:344
  280.6 9.2 %collective-permute-start.41 = (bf16[128,1024]{1,0:T(8,128)(2,1)S(1)}, bf16[128,1024]{1,0:T(8,128)(2,1)S(1)}, u32[]{:S(2)}, u32[]{:S(2)}) collective-permute-start(bf16[128,1024]{1,0:T(8,128)(2,1)S(1)} %fusion.19), channel_id=1, source_target_pairs={{0,3},{1,2},{2,1},{3,0},{4,7},{5,6},{6,5},{7,4},{8,11},{9,10},{10,... | collective-permute-start | bytes 786440 | tf_op jit(solution)/shard_map/ppermute | solution.py:377
  283.1 7.9 %collective-permute-start.40 = (bf16[128,1024]{1,0:T(8,128)(2,1)S(1)}, bf16[128,1024]{1,0:T(8,128)(2,1)S(1)}, u32[]{:S(2)}, u32[]{:S(2)}) collective-permute-start(bf16[128,1024]{1,0:T(8,128)(2,1)S(1)} %fusion.19), channel_id=1, source_target_pairs={{0,2},{1,3},{2,0},{3,1},{4,6},{5,7},{6,4},{7,5},{8,10},{9,11},{10,... | collective-permute-start | bytes 786440 | tf_op jit(solution)/shard_map/ppermute | solution.py:377
  283.1 8.8 %collective-permute-start.39 = (bf16[128,1024]{1,0:T(8,128)(2,1)S(1)}, bf16[128,1024]{1,0:T(8,128)(2,1)S(1)}, u32[]{:S(2)}, u32[]{:S(2)}) collective-permute-start(bf16[128,1024]{1,0:T(8,128)(2,1)S(1)} %fusion.19), channel_id=1, source_target_pairs={{0,1},{1,0},{2,3},{3,2},{4,5},{5,4},{6,7},{7,6},{8,9},{9,8},{10,11... | collective-permute-start | bytes 786440 | tf_op jit(solution)/shard_map/ppermute | solution.py:377
  (7 other events, 38.9 us)
where the time goes:
time: 296 us; the launch traced here: 293 us
  waiting for transfers between devices  109 us (37%)
  starting transfers between devices  86.2 us (29%)
  Pallas kernels  55.8 us (19%)
  other arithmetic  22.2 us (8%)
  local copies, waits for them, and re-layouts  17.4 us (6%)
    ppermute x18, waiting for transfers between devices, collect(): got = lax.ppermute(high, AXES, stage_pairs(part, stage))  52.1 us
    ppermute x18, starting transfers between devices, collect(): got = lax.ppermute(high, AXES, stage_pairs(part, stage))  50.9 us
    ppermute x18, waiting for transfers between devices, spread(): lax.ppermute(held[p], AXES, stage_pairs(p, stage))  48.8 us
    pallas_call x3, Pallas kernels, find_sums(): pl.pallas_call(functools.partial(down_kernel, part), in_specs=[smem, smem...  30.8 us
    ppermute x18, starting transfers between devices, spread(): lax.ppermute(held[p], AXES, stage_pairs(p, stage))  25.8 us
    pallas_call x1, Pallas kernels, find_hidden(): pl.pallas_call(hidden_kernel, in_specs=[smem, smem, vmem, vmem] + [anywhe...  25 us
    convert_element_type x15, other arithmetic, add(): return (a.astype(jnp.float32) + b.astype(jnp.float32)).astype(jnp.bfloat16)  11.8 us
    unnamed x28, local copies, waits for them, and re-layouts  7.57 us
  transfers between devices with their start and end apart: 43, of which 25 were waited for; matrix products, arithmetic and copies ran while one was open for 13% of the time, Pallas kernels for 7%

commit v1 on v0

--- a/solution.py
+++ b/solution.py
@@ -24,8 +24,11 @@
 ROWS = (352, 336, 336)
 ROW_AT = (0, 352, 688)
 PARTS = len(ROWS)
+BACK = (352, 336, 336)
+BACK_AT = (0, 352, 688)
 PAIRS = BLOCKS // 2
 GROUPS = 4
+AHEAD = 4
 SLOT_STEP = SLOTS // GROUPS
 GROUP_ROWS = 2 * SLOT_STEP
 TILE = PAIRS * GROUP_ROWS
@@ -33,7 +36,7 @@
 
 
 def tiles_of(part):
-    first, last = ROW_AT[part], ROW_AT[part] + ROWS[part]
+    first, last = BACK_AT[part], BACK_AT[part] + BACK[part]
     found = []
     for tile in range(first // TOK, -(-last // TOK)):
         start, stop = max(first - tile * TOK, 0), min(last - tile * TOK, TOK)
@@ -42,7 +45,7 @@
 
 
 def link_of(part, core, stage):
-    return LINKS[(2 * part + core + stage) % STAGES]
+    return LINKS[(2 * part + 1 - core + stage) % STAGES]
 
 
 def device_number(at):
@@ -121,17 +124,18 @@
                     def _(part=part, j=j, to=to, sem=sem):
                         pltpu.make_async_copy(high[part].at[j - HALF], to, sem).start()
 
-    fetch(0, 0, True)
+    for pair in range(AHEAD - 1):
+        fetch(pair, pair, True)
     for copy in weight_copies(g_own, u_own, 0, 0):
         copy.start()
 
     @pl.loop(0, PAIRS)
     def _(pair):
-        slot = lax.rem(pair, 2)
-
-        @pl.when(pair + 1 < PAIRS)
+        slot = lax.rem(pair, AHEAD)
+
+        @pl.when(pair + AHEAD - 1 < PAIRS)
         def _():
-            fetch(pair + 1, 1 - slot, True)
+            fetch(pair + AHEAD - 1, lax.rem(pair + AHEAD - 1, AHEAD), True)
 
         fetch(pair, slot, False)
         at = pl.multiple_of(pair * GROUP_ROWS, GROUP_ROWS)
@@ -186,12 +190,12 @@
         out_shape=jax.ShapeDtypeStruct((CHIP_EXPERTS, n, ff), jnp.bfloat16),
         scratch_shapes=[
             pltpu.VMEM((CHIP_EXPERTS, n, 4 * WIDTH), jnp.bfloat16),
-            pltpu.VMEM((2, 2, 4, TILES * TOK, LANES), jnp.bfloat16),
+            pltpu.VMEM((AHEAD, 2, 4, TILES * TOK, LANES), jnp.bfloat16),
             pltpu.VMEM((2, 4 * WIDTH, 2 * ff), jnp.bfloat16),
-            pltpu.SemaphoreType.DMA((2, 8 * PARTS)),
+            pltpu.SemaphoreType.DMA((AHEAD, 8 * PARTS)),
             pltpu.SemaphoreType.DMA((2, 2)),
         ],
-        compiler_params=pltpu.CompilerParams(vmem_limit_bytes=48 << 20),
+        compiler_params=pltpu.CompilerParams(vmem_limit_bytes=44 << 20),
         cost_estimate=pl.CostEstimate(
             flops=2 * 2048 * 4096 * 1024, bytes_accessed=100 << 20, transcendentals=2048 * 384
         ),
@@ -277,13 +281,13 @@
         functools.partial(down_kernel, part),
         in_specs=[smem, smem, vmem, vmem, anywhere, anywhere],
         out_specs=[vmem] * 2,
-        out_shape=[jax.ShapeDtypeStruct((HALF + 1, ROWS[part], LANES), jnp.bfloat16)] * 2,
+        out_shape=[jax.ShapeDtypeStruct((HALF + 1, BACK[part], LANES), jnp.bfloat16)] * 2,
         scratch_shapes=[
             pltpu.VMEM((CHIP_EXPERTS, ff, 4 * f), jnp.bfloat16),
             pltpu.VMEM((CHIP_EXPERTS, n, 4 * f), jnp.bfloat16),
             pltpu.SemaphoreType.DMA((CHIP_EXPERTS, 4)),
         ],
-        compiler_params=pltpu.CompilerParams(vmem_limit_bytes=32 << 20),
+        compiler_params=pltpu.CompilerParams(vmem_limit_bytes=28 << 20),
         cost_estimate=pl.CostEstimate(
             flops=2 * 2048 * 4 * f * (ff + 256), bytes_accessed=40 << 20, transcendentals=0
         ),

time: 296 us -> 291 us (0.983)
  waiting for transfers between devices: 109 us -> 139 us
  starting transfers between devices: 86.2 us -> 56.3 us
  Pallas kernels: 55.8 us -> 51.4 us
    ppermute x18, starting transfers between devices: 50.9 us -> 23.7 us  [collect(): got = lax.ppermute(high, AXES, stage_pairs(part, stage))]
    ppermute x18, waiting for transfers between devices: 52.1 us -> 77.7 us  [collect(): got = lax.ppermute(high, AXES, stage_pairs(part, stage))]
    ppermute x18, waiting for transfers between devices: 48.8 us -> 52.9 us  [spread(): lax.ppermute(held[p], AXES, stage_pairs(p, stage))]
    ppermute x18, starting transfers between devices: 25.8 us -> 21.7 us  [spread(): lax.ppermute(held[p], AXES, stage_pairs(p, stage))]
    pallas_call x3, Pallas kernels: 30.8 us -> 27.7 us  [find_sums(): pl.pallas_call(functools.partial(down_kernel, part), in_specs=[smem, smem...]
  transfers between devices with their start and end apart: 43 -> 43, of which waited for: 25 -> 27; matrix products, arithmetic and copies ran while one was open for 13% -> 13% of each run, Pallas kernels for 7% -> 6%
where the time goes in v1:
time: 291 us; the launch traced here: 289 us
  waiting for transfers between devices  139 us (48%)
  starting transfers between devices  56.3 us (19%)
  Pallas kernels  51.4 us (18%)
  other arithmetic  22 us (8%)
  local copies, waits for them, and re-layouts  17.4 us (6%)
    ppermute x18, waiting for transfers between devices, collect(): got = lax.ppermute(high, AXES, stage_pairs(part, stage))  77.7 us
    ppermute x18, waiting for transfers between devices, spread(): lax.ppermute(held[p], AXES, stage_pairs(p, stage))  52.9 us
    pallas_call x3, Pallas kernels, find_sums(): pl.pallas_call(functools.partial(down_kernel, part), in_specs=[smem, smem...  27.7 us
    pallas_call x1, Pallas kernels, find_hidden(): pl.pallas_call(hidden_kernel, in_specs=[smem, smem, vmem, vmem] + [anywhe...  23.7 us
    ppermute x18, starting transfers between devices, collect(): got = lax.ppermute(high, AXES, stage_pairs(part, stage))  23.7 us
    ppermute x18, starting transfers between devices, spread(): lax.ppermute(held[p], AXES, stage_pairs(p, stage))  21.7 us
    convert_element_type x15, other arithmetic, add(): return (a.astype(jnp.float32) + b.astype(jnp.float32)).astype(jnp.bfloat16)  11.6 us
    unnamed x28, local copies, waits for them, and re-layouts  7.57 us
  transfers between devices with their start and end apart: 43, of which 27 were waited for; matrix products, arithmetic and copies ran while one was open for 13% of the time, Pallas kernels for 6%

profile of v1, /device:TPU:0, one launch (start us, length us, event | category | flops | bytes accessed | tf_op | source)
XLA Modules:
  0.0 288.9 jit_solution(11941588504773619690)
XLA Ops:
  1.7 2.9 %collective-permute-start.2 = (bf16[1,336,128]{2,1,0:T(8,128)(2,1)S(1)}, bf16[1,336,128]{2,1,0:T(8,128)(2,1)S(1)}, u32[]{:S(2)}, u32[]{:S(2)}) collective-permute-start(bf16[1,336,128]{2,1,0:T(8,128)(2,1)S(1)} %get-tuple-element.81), channel_id=1, source_target_pairs={{0,3},{1,2},{2,1},{3,0},{4,12},{5,13},{6,14},{7,15},{8,11},{9,10},... | collective-permute-start | bytes 258056 | tf_op jit(solution)/shard_map/ppermute | solution.py:332
  4.7 3.0 %collective-permute-start = (bf16[1,352,128]{2,1,0:T(8,128)(2,1)S(1)}, bf16[1,352,128]{2,1,0:T(8,128)(2,1)S(1)}, u32[]{:S(2)}, u32[]{:S(2)}) collective-permute-start(bf16[1,352,128]{2,1,0:T(8,128)(2,1)S(1)} %slice_bitcast_fusion), channel_id=1, source_target_pairs={{0,96},{1,97},{2,98},{3,99},{4,5},{5,4},{6,7},{7,6},{8,104},{9,105... | collective-permute-start | bytes 270344 | tf_op jit(solution)/shard_map/ppermute | solution.py:332
  7.7 4.0 %collective-permute-start.4 = (bf16[1,336,128]{2,1,0:T(8,128)(2,1)S(1)}, bf16[1,336,128]{2,1,0:T(8,128)(2,1)S(1)}, u32[]{:S(2)}, u32[]{:S(2)}) collective-permute-start(bf16[1,336,128]{2,1,0:T(8,128)(2,1)S(1)} %get-tuple-element.80), channel_id=1, source_target_pairs={{0,24},{1,25},{2,26},{3,27},{4,36},{5,37},{6,38},{7,39},{8,16},{9,... | collective-permute-start | bytes 258056 | tf_op jit(solution)/shard_map/ppermute | solution.py:332
  12.0 3.1 %collective-permute-done.4 = bf16[1,336,128]{2,1,0:T(8,128)(2,1)S(1)} collective-permute-done((bf16[1,336,128]{2,1,0:T(8,128)(2,1)S(1)}, bf16[1,336,128]{2,1,0:T(8,128)(2,1)S(1)}, u32[]{:S(2)}, u32[]{:S(2)}) %collective-permute-start.4) | collective-permute-done | bytes 86048 | tf_op jit(solution)/shard_map/ppermute | solution.py:332
  15.3 1.9 collective-permute-done.3
  17.3 3.3 %collective-permute-done.5 = bf16[2,336,128]{2,1,0:T(8,128)(2,1)S(1)} collective-permute-done((bf16[2,336,128]{2,1,0:T(8,128)(2,1)S(1)}, bf16[2,336,128]{2,1,0:T(8,128)(2,1)S(1)}, u32[]{:S(2)}, u32[]{:S(2)}) %collective-permute-start.5) | collective-permute-done | bytes 172064 | tf_op jit(solution)/shard_map/ppermute | solution.py:332
  21.0 2.6 copy-done.9
  23.6 3.4 %collective-permute-start.8 = (bf16[4,336,128]{2,1,0:T(8,128)(2,1)S(1)}, bf16[4,336,128]{2,1,0:T(8,128)(2,1)S(1)}, u32[]{:S(2)}, u32[]{:S(2)}) collective-permute-start(bf16[4,336,128]{2,1,0:T(8,128)(2,1)S(1)} %pad_maximum_fusion.9), channel_id=1, source_target_pairs={{0,24},{1,25},{2,26},{3,27},{4,36},{5,37},{6,38},{7,39},{8,16},{9,... | collective-permute-start | bytes 1032200 | tf_op jit(solution)/shard_map/ppermute | solution.py:332
  27.8 4.5 %collective-permute-done.8 = bf16[4,336,128]{2,1,0:T(8,128)(2,1)S(1)} collective-permute-done((bf16[4,336,128]{2,1,0:T(8,128)(2,1)S(1)}, bf16[4,336,128]{2,1,0:T(8,128)(2,1)S(1)}, u32[]{:S(2)}, u32[]{:S(2)}) %collective-permute-start.8) | collective-permute-done | bytes 344096 | tf_op jit(solution)/shard_map/ppermute | solution.py:332
  32.3 3.2 %collective-permute-done.9 = bf16[4,336,128]{2,1,0:T(8,128)(2,1)S(1)} collective-permute-done((bf16[4,336,128]{2,1,0:T(8,128)(2,1)S(1)}, bf16[4,336,128]{2,1,0:T(8,128)(2,1)S(1)}, u32[]{:S(2)}, u32[]{:S(2)}) %collective-permute-start.9) | collective-permute-done | bytes 344096 | tf_op jit(solution)/shard_map/ppermute | solution.py:332
  35.8 1.8 collective-permute-start.12
  38.4 6.5 %all-to-all-start = ((f32[16,4,128]{2,1,0:T(4,128)}), f32[16,4,128]{2,1,0:T(4,128)}, u32[]{:S(2)}, u32[]{:S(2)}) async-start(f32[16,4,128]{2,1,0:T(4,128)} %bitcast.8), calls=%async_computation | async-start | bytes 65536 | tf_op jit(solution)/shard_map/all_to_all | solution.py:368
  44.9 1.9 collective-permute-done.12
  51.3 1.3 all-to-all-done
  52.6 1.3 collective-permute-start.17
  53.9 2.2 collective-permute-start.15
  56.3 2.5 constant_dynamic-update-slice_fusion.3
  61.2 11.1 %collective-permute-done.17 = bf16[16,336,128]{2,1,0:T(8,128)(2,1)S(1)} collective-permute-done((bf16[16,336,128]{2,1,0:T(8,128)(2,1)}, bf16[16,336,128]{2,1,0:T(8,128)(2,1)S(1)}, u32[]{:S(2)}, u32[]{:S(2)}) %collective-permute-start.17) | collective-permute-done | bytes 1376288 | tf_op jit(solution)/shard_map/ppermute | solution.py:332
  74.1 1.3 constant_dynamic-update-slice_fusion.lo0
  80.9 1.9 copy.48
  82.7 1.9 and_convert_fusion
  86.5 1.9 fusion.30.put
  88.4 18.4 %collective-permute-done.18.hi1 = bf16[32,336,128]{2,1,0:T(8,128)(2,1)} collective-permute-done((bf16[32,336,128]{2,1,0:T(8,128)(2,1)}, bf16[32,336,128]{2,1,0:T(8,128)(2,1)}, u32[]{:S(2)}, u32[]{:S(2)}) %collective-permute-start.18) | collective-permute-done | bytes 2752544 | tf_op jit(solution)/shard_map/ppermute | solution.py:332
  106.9 4.3 %collective-permute-done.20.hi2 = bf16[32,336,128]{2,1,0:T(8,128)(2,1)} collective-permute-done((bf16[32,336,128]{2,1,0:T(8,128)(2,1)}, bf16[32,336,128]{2,1,0:T(8,128)(2,1)}, u32[]{:S(2)}, u32[]{:S(2)}) %collective-permute-start.20) | collective-permute-done | bytes 2752544 | tf_op jit(solution)/shard_map/ppermute | solution.py:332
  111.1 23.7 %hidden.1 = bf16[4,512,384]{2,1,0:T(8,128)(2,1)S(1)} custom-call(s32[192]{0:T(256)S(1)} %bitcast.53, s32[4]{0:T(128)S(1)} %fusion.23.groups, bf16[8,256,256]{2,1,0:T(8,128)(2,1)S(1)} %copy.53.pick, f32[4,512,1]{2,1,0:T(8,128)S(1)} %reshape.72.weight, bf16[32,352,128]{2,1,0:T(8,128)(2,1)} %constant_dynamic-update-slice_fusion.lo0, ...), custom_call_target="tpu_custom_call" | custom-call | flops 17179869184 | bytes 104857600 | tf_op jit(solution)/shard_map/hidden/pallas_call | solution.py:186
  134.9 9.1 %sums.5 = (bf16[33,336,128]{2,1,0:T(8,128)(2,1)S(1)}, bf16[33,336,128]{2,1,0:T(8,128)(2,1)S(1)}) custom-call(s32[4]{0:T(128)S(1)} %fusion.23.groups, s32[192]{0:T(256)S(1)} %bitcast.54, bf16[8,256,256]{2,1,0:T(8,128)(2,1)S(1)} %fusion.30.put, bf16[4,512,384]{2,1,0:T(8,128)(2,1)S(1)} %hidden.1, bf16[2,384,4096]{2,1,0:T(8,128)(2,1)} %d_own.5, ...), custom_call_target="tpu_custom_call" | custom-call | flops 4026531840 | bytes 41943040 | tf_op jit(solution)/shard_map/sums/pallas_call | solution.py:280
  144.0 9.6 %sums.4 = (bf16[33,336,128]{2,1,0:T(8,128)(2,1)S(1)}, bf16[33,336,128]{2,1,0:T(8,128)(2,1)S(1)}) custom-call(s32[4]{0:T(128)S(1)} %fusion.23.groups, s32[192]{0:T(256)S(1)} %bitcast.55, bf16[8,256,256]{2,1,0:T(8,128)(2,1)S(1)} %fusion.30.put, bf16[4,512,384]{2,1,0:T(8,128)(2,1)S(1)} %hidden.1, bf16[2,384,4096]{2,1,0:T(8,128)(2,1)} %d_own.5, ...), custom_call_target="tpu_custom_call" | custom-call | flops 5368709120 | bytes 41943040 | tf_op jit(solution)/shard_map/sums/pallas_call | solution.py:280
  153.7 3.8 %collective-permute-start.27 = (bf16[33,336,128]{2,1,0:T(8,128)(2,1)S(1)}, bf16[33,336,128]{2,1,0:T(8,128)(2,1)}, u32[]{:S(2)}, u32[]{:S(2)}) collective-permute-start(bf16[33,336,128]{2,1,0:T(8,128)(2,1)S(1)} %get-tuple-element.49), channel_id=1, source_target_pairs={{0,8},{1,9},{2,10},{3,11},{4,100},{5,101},{6,102},{7,103},{8,0},{9... | collective-permute-start | bytes 8515592 | tf_op jit(solution)/shard_map/ppermute | solution.py:348
  157.4 9.0 %sums.3 = (bf16[33,352,128]{2,1,0:T(8,128)(2,1)S(1)}, bf16[33,352,128]{2,1,0:T(8,128)(2,1)S(1)}) custom-call(s32[4]{0:T(128)S(1)} %fusion.23.groups, s32[192]{0:T(256)S(1)} %bitcast.56, bf16[8,256,256]{2,1,0:T(8,128)(2,1)S(1)} %fusion.30.put, bf16[4,512,384]{2,1,0:T(8,128)(2,1)S(1)} %hidden.1, bf16[2,384,4096]{2,1,0:T(8,128)(2,1)} %d_own.5, ...), custom_call_target="tpu_custom_call" | custom-call | flops 4026531840 | bytes 41943040 | tf_op jit(solution)/shard_map/sums/pallas_call | solution.py:280
  167.2 10.9 %collective-permute-done.33 = bf16[33,336,128]{2,1,0:T(8,128)(2,1)} collective-permute-done((bf16[33,336,128]{2,1,0:T(8,128)(2,1)S(1)}, bf16[33,336,128]{2,1,0:T(8,128)(2,1)}, u32[]{:S(2)}, u32[]{:S(2)}) %collective-permute-start.33) | collective-permute-done | bytes 2838560 | tf_op jit(solution)/shard_map/ppermute | solution.py:348
  178.1 2.5 add_convert_fusion.3
  181.7 13.6 %collective-permute-done.27 = bf16[33,336,128]{2,1,0:T(8,128)(2,1)} collective-permute-done((bf16[33,336,128]{2,1,0:T(8,128)(2,1)S(1)}, bf16[33,336,128]{2,1,0:T(8,128)(2,1)}, u32[]{:S(2)}, u32[]{:S(2)}) %collective-permute-start.27) | collective-permute-done | bytes 2838560 | tf_op jit(solution)/shard_map/ppermute | solution.py:348
  195.3 2.5 add_convert_fusion.5
  197.9 10.8 %collective-permute-done.21 = bf16[33,352,128]{2,1,0:T(8,128)(2,1)S(1)} collective-permute-done((bf16[33,352,128]{2,1,0:T(8,128)(2,1)S(1)}, bf16[33,352,128]{2,1,0:T(8,128)(2,1)S(1)}, u32[]{:S(2)}, u32[]{:S(2)}) %collective-permute-start.21) | collective-permute-done | bytes 2973728 | tf_op jit(solution)/shard_map/ppermute | solution.py:348
  210.8 2.0 collective-permute-start.35
  212.8 12.0 %collective-permute-done.28 = bf16[16,336,128]{2,1,0:T(8,128)(2,1)S(1)} collective-permute-done((bf16[16,336,128]{2,1,0:T(8,128)(2,1)S(1)}, bf16[16,336,128]{2,1,0:T(8,128)(2,1)S(1)}, u32[]{:S(2)}, u32[]{:S(2)}) %collective-permute-start.28) | collective-permute-done | bytes 1376288 | tf_op jit(solution)/shard_map/ppermute | solution.py:348
  226.0 2.6 collective-permute-start.29
  228.6 8.6 %collective-permute-done.22 = bf16[16,352,128]{2,1,0:T(8,128)(2,1)S(1)} collective-permute-done((bf16[16,352,128]{2,1,0:T(8,128)(2,1)S(1)}, bf16[16,352,128]{2,1,0:T(8,128)(2,1)S(1)}, u32[]{:S(2)}, u32[]{:S(2)}) %collective-permute-start.22) | collective-permute-done | bytes 1441824 | tf_op jit(solution)/shard_map/ppermute | solution.py:348
  237.5 6.8 %collective-permute-start.23 = (bf16[8,352,128]{2,1,0:T(8,128)(2,1)S(1)}, bf16[8,352,128]{2,1,0:T(8,128)(2,1)S(1)}, u32[]{:S(2)}, u32[]{:S(2)}) collective-permute-start(bf16[8,352,128]{2,1,0:T(8,128)(2,1)S(1)} %get-tuple-element.59), channel_id=1, source_target_pairs={{0,32},{1,33},{2,34},{3,35},{4,7},{5,6},{6,5},{7,4},{8,40},{9,41},... | collective-permute-start | bytes 2162696 | tf_op jit(solution)/shard_map/ppermute | solution.py:348
  247.0 7.4 %collective-permute-done.23 = bf16[8,352,128]{2,1,0:T(8,128)(2,1)S(1)} collective-permute-done((bf16[8,352,128]{2,1,0:T(8,128)(2,1)S(1)}, bf16[8,352,128]{2,1,0:T(8,128)(2,1)S(1)}, u32[]{:S(2)}, u32[]{:S(2)}) %collective-permute-start.23) | collective-permute-done | bytes 720928 | tf_op jit(solution)/shard_map/ppermute | solution.py:348
  256.1 2.1 collective-permute-start.31
  258.2 2.2 collective-permute-done.37
  261.6 2.9 collective-permute-start.32
  264.6 1.5 collective-permute-done.38
  266.2 3.9 %collective-permute-done.25 = bf16[2,352,128]{2,1,0:T(8,128)(2,1)S(1)} collective-permute-done((bf16[2,352,128]{2,1,0:T(8,128)(2,1)S(1)}, bf16[2,352,128]{2,1,0:T(8,128)(2,1)S(1)}, u32[]{:S(2)}, u32[]{:S(2)}) %collective-permute-start.25) | collective-permute-done | bytes 180256 | tf_op jit(solution)/shard_map/ppermute | solution.py:348
  270.3 5.7 %collective-permute-done.26 = bf16[1,352,128]{2,1,0:T(8,128)(2,1)S(1)} collective-permute-done((bf16[1,352,128]{2,1,0:T(8,128)(2,1)S(1)}, bf16[1,352,128]{2,1,0:T(8,128)(2,1)S(1)}, u32[]{:S(2)}, u32[]{:S(2)}) %collective-permute-start.26) | collective-permute-done | bytes 90144 | tf_op jit(solution)/shard_map/ppermute | solution.py:348
  276.7 2.4 collective-permute-start.40
  280.5 6.2 %collective-permute-done.41 = bf16[128,1024]{1,0:T(8,128)(2,1)S(1)} collective-permute-done((bf16[128,1024]{1,0:T(8,128)(2,1)S(1)}, bf16[128,1024]{1,0:T(8,128)(2,1)S(1)}, u32[]{:S(2)}, u32[]{:S(2)}) %collective-permute-start.41) | collective-permute-done | bytes 262176 | tf_op jit(solution)/shard_map/ppermute | solution.py:381
  (140 shorter events, 35.7 us)
Async XLA Ops:
  0.6 20.2 %collective-permute-start.6 = (bf16[2,4096,384]{2,1,0:T(8,128)(2,1)}, bf16[2,4096,384]{2,1,0:T(8,128)(2,1)S(1)}, u32[]{:S(2)}, u32[]{:S(2)}) collective-permute-start(bf16[2,4096,384]{2,1,0:T(8,128)(2,1)} %g_own.1), channel_id=1, source_target_pairs={{0,4},{1,5},{2,6},{3,7},{4,0},{5,1},{6,2},{7,3},{8,12},{9,13},{10,... | collective-permute-start | bytes 18874376 | tf_op jit(solution)/shard_map/ppermute | solution.py:331
  1.7 10.0 %collective-permute-start.2 = (bf16[1,336,128]{2,1,0:T(8,128)(2,1)S(1)}, bf16[1,336,128]{2,1,0:T(8,128)(2,1)S(1)}, u32[]{:S(2)}, u32[]{:S(2)}) collective-permute-start(bf16[1,336,128]{2,1,0:T(8,128)(2,1)S(1)} %get-tuple-element.81), channel_id=1, source_target_pairs={{0,3},{1,2},{2,1},{3,0},{4,12},{5,13},{6,14},{7,15},{8,11},{9,10},... | collective-permute-start | bytes 258056 | tf_op jit(solution)/shard_map/ppermute | solution.py:332
  4.7 10.5 %collective-permute-start = (bf16[1,352,128]{2,1,0:T(8,128)(2,1)S(1)}, bf16[1,352,128]{2,1,0:T(8,128)(2,1)S(1)}, u32[]{:S(2)}, u32[]{:S(2)}) collective-permute-start(bf16[1,352,128]{2,1,0:T(8,128)(2,1)S(1)} %slice_bitcast_fusion), channel_id=1, source_target_pairs={{0,96},{1,97},{2,98},{3,99},{4,5},{5,4},{6,7},{7,6},{8,104},{9,105... | collective-permute-start | bytes 270344 | tf_op jit(solution)/shard_map/ppermute | solution.py:332
  7.7 7.4 %collective-permute-start.4 = (bf16[1,336,128]{2,1,0:T(8,128)(2,1)S(1)}, bf16[1,336,128]{2,1,0:T(8,128)(2,1)S(1)}, u32[]{:S(2)}, u32[]{:S(2)}) collective-permute-start(bf16[1,336,128]{2,1,0:T(8,128)(2,1)S(1)} %get-tuple-element.80), channel_id=1, source_target_pairs={{0,24},{1,25},{2,26},{3,27},{4,36},{5,37},{6,38},{7,39},{8,16},{9,... | collective-permute-start | bytes 258056 | tf_op jit(solution)/shard_map/ppermute | solution.py:332
  11.8 5.5 %collective-permute-start.3 = (bf16[2,336,128]{2,1,0:T(8,128)(2,1)S(1)}, bf16[2,336,128]{2,1,0:T(8,128)(2,1)S(1)}, u32[]{:S(2)}, u32[]{:S(2)}) collective-permute-start(bf16[2,336,128]{2,1,0:T(8,128)(2,1)S(1)} %pad_maximum_fusion.13), channel_id=1, source_target_pairs={{0,32},{1,33},{2,34},{3,35},{4,7},{5,6},{6,5},{7,4},{8,40},{9,41},... | collective-permute-start | bytes 516104 | tf_op jit(solution)/shard_map/ppermute | solution.py:332
  15.1 5.5 %collective-permute-start.5 = (bf16[2,336,128]{2,1,0:T(8,128)(2,1)S(1)}, bf16[2,336,128]{2,1,0:T(8,128)(2,1)S(1)}, u32[]{:S(2)}, u32[]{:S(2)}) collective-permute-start(bf16[2,336,128]{2,1,0:T(8,128)(2,1)S(1)} %pad_maximum_fusion.14), channel_id=1, source_target_pairs={{0,1},{1,0},{2,3},{3,2},{4,28},{5,29},{6,30},{7,31},{8,9},{9,8},{1... | collective-permute-start | bytes 516104 | tf_op jit(solution)/shard_map/ppermute | solution.py:332
  15.2 5.6 %collective-permute-start.1 = (bf16[2,352,128]{2,1,0:T(8,128)(2,1)S(1)}, bf16[2,352,128]{2,1,0:T(8,128)(2,1)S(1)}, u32[]{:S(2)}, u32[]{:S(2)}) collective-permute-start(bf16[2,352,128]{2,1,0:T(8,128)(2,1)S(1)} %pad_maximum_fusion.11), channel_id=1, source_target_pairs={{0,8},{1,9},{2,10},{3,11},{4,100},{5,101},{6,102},{7,103},{8,0},{9... | collective-permute-start | bytes 540680 | tf_op jit(solution)/shard_map/ppermute | solution.py:332
  20.8 16.8 %copy-start.11 = (s32[128]{0:T(128)S(1)}, s32[128]{0:T(128)}, u32[]{:S(2)}) copy-start(s32[128]{0:T(128)} %param.14) | copy-start | bytes 1540
  20.8 16.8 %copy-start.6 = (f32[128,8]{0,1:T(8,128)S(1)}, f32[128,8]{0,1:T(8,128)}, u32[]{:S(2)}) copy-start(f32[128,8]{0,1:T(8,128)} %param.16) | copy-start | bytes 12292
  20.9 16.8 %copy-start.7 = (s32[128,8]{0,1:T(8,128)S(1)}, s32[128,8]{0,1:T(8,128)}, u32[]{:S(2)}) copy-start(s32[128,8]{0,1:T(8,128)} %param.15) | copy-start | bytes 12292
  20.9 14.8 %collective-permute-start.10 = (bf16[2,4096,384]{2,1,0:T(8,128)(2,1)}, bf16[2,4096,384]{2,1,0:T(8,128)(2,1)S(1)}, u32[]{:S(2)}, u32[]{:S(2)}) collective-permute-start(bf16[2,4096,384]{2,1,0:T(8,128)(2,1)} %u_own.1), channel_id=1, source_target_pairs={{0,4},{1,5},{2,6},{3,7},{4,0},{5,1},{6,2},{7,3},{8,12},{9,13},{10,... | collective-permute-start | bytes 18874376 | tf_op jit(solution)/shard_map/ppermute | solution.py:331
  23.6 8.6 %collective-permute-start.8 = (bf16[4,336,128]{2,1,0:T(8,128)(2,1)S(1)}, bf16[4,336,128]{2,1,0:T(8,128)(2,1)S(1)}, u32[]{:S(2)}, u32[]{:S(2)}) collective-permute-start(bf16[4,336,128]{2,1,0:T(8,128)(2,1)S(1)} %pad_maximum_fusion.9), channel_id=1, source_target_pairs={{0,24},{1,25},{2,26},{3,27},{4,36},{5,37},{6,38},{7,39},{8,16},{9,... | collective-permute-start | bytes 1032200 | tf_op jit(solution)/shard_map/ppermute | solution.py:332
  27.0 8.5 %collective-permute-start.9 = (bf16[4,336,128]{2,1,0:T(8,128)(2,1)S(1)}, bf16[4,336,128]{2,1,0:T(8,128)(2,1)S(1)}, u32[]{:S(2)}, u32[]{:S(2)}) collective-permute-start(bf16[4,336,128]{2,1,0:T(8,128)(2,1)S(1)} %pad_maximum_fusion.10), channel_id=1, source_target_pairs={{0,96},{1,97},{2,98},{3,99},{4,5},{5,4},{6,7},{7,6},{8,104},{9,105... | collective-permute-start | bytes 1032200 | tf_op jit(solution)/shard_map/ppermute | solution.py:332
  27.0 8.6 %collective-permute-start.7 = (bf16[4,352,128]{2,1,0:T(8,128)(2,1)S(1)}, bf16[4,352,128]{2,1,0:T(8,128)(2,1)S(1)}, u32[]{:S(2)}, u32[]{:S(2)}) collective-permute-start(bf16[4,352,128]{2,1,0:T(8,128)(2,1)S(1)} %pad_maximum_fusion.8), channel_id=1, source_target_pairs={{0,3},{1,2},{2,1},{3,0},{4,12},{5,13},{6,14},{7,15},{8,11},{9,10},... | collective-permute-start | bytes 1081352 | tf_op jit(solution)/shard_map/ppermute | solution.py:332
  35.7 16.9 %collective-permute-start.14 = (bf16[2,384,4096]{2,1,0:T(8,128)(2,1)}, bf16[2,384,4096]{2,1,0:T(8,128)(2,1)}, u32[]{:S(2)}, u32[]{:S(2)}) collective-permute-start(bf16[2,384,4096]{2,1,0:T(8,128)(2,1)} %d_own.5), channel_id=1, source_target_pairs={{0,4},{1,5},{2,6},{3,7},{4,0},{5,1},{6,2},{7,3},{8,12},{9,13},{10,... | collective-permute-start | bytes 18874376 | tf_op jit(solution)/shard_map/ppermute | solution.py:331
  35.8 11.0 %collective-permute-start.12 = (bf16[8,336,128]{2,1,0:T(8,128)(2,1)S(1)}, bf16[8,336,128]{2,1,0:T(8,128)(2,1)S(1)}, u32[]{:S(2)}, u32[]{:S(2)}) collective-permute-start(bf16[8,336,128]{2,1,0:T(8,128)(2,1)S(1)} %pad_maximum_fusion.5), channel_id=1, source_target_pairs={{0,1},{1,0},{2,3},{3,2},{4,28},{5,29},{6,30},{7,31},{8,9},{9,8},{1... | collective-permute-start | bytes 2064392 | tf_op jit(solution)/shard_map/ppermute | solution.py:332
  37.7 11.1 %collective-permute-start.13 = (bf16[8,336,128]{2,1,0:T(8,128)(2,1)S(1)}, bf16[8,336,128]{2,1,0:T(8,128)(2,1)}, u32[]{:S(2)}, u32[]{:S(2)}) collective-permute-start(bf16[8,336,128]{2,1,0:T(8,128)(2,1)S(1)} %pad_maximum_fusion.6), channel_id=1, source_target_pairs={{0,8},{1,9},{2,10},{3,11},{4,100},{5,101},{6,102},{7,103},{8,0},{9... | collective-permute-start | bytes 2064392 | tf_op jit(solution)/shard_map/ppermute | solution.py:332
  37.7 12.4 %collective-permute-start.11 = (bf16[8,352,128]{2,1,0:T(8,128)(2,1)S(1)}, bf16[8,352,128]{2,1,0:T(8,128)(2,1)}, u32[]{:S(2)}, u32[]{:S(2)}) collective-permute-start(bf16[8,352,128]{2,1,0:T(8,128)(2,1)S(1)} %pad_maximum_fusion.4), channel_id=1, source_target_pairs={{0,32},{1,33},{2,34},{3,35},{4,7},{5,6},{6,5},{7,4},{8,40},{9,41},... | collective-permute-start | bytes 2162696 | tf_op jit(solution)/shard_map/ppermute | solution.py:332
  38.4 14.1 %all-to-all-start = ((f32[16,4,128]{2,1,0:T(4,128)}), f32[16,4,128]{2,1,0:T(4,128)}, u32[]{:S(2)}, u32[]{:S(2)}) async-start(f32[16,4,128]{2,1,0:T(4,128)} %bitcast.8), calls=%async_computation | async-start | bytes 65536 | tf_op jit(solution)/shard_map/all_to_all | solution.py:368
  52.6 19.7 %collective-permute-start.17 = (bf16[16,336,128]{2,1,0:T(8,128)(2,1)}, bf16[16,336,128]{2,1,0:T(8,128)(2,1)S(1)}, u32[]{:S(2)}, u32[]{:S(2)}) collective-permute-start(bf16[16,336,128]{2,1,0:T(8,128)(2,1)} %pad_maximum_fusion.1), channel_id=1, source_target_pairs={{0,96},{1,97},{2,98},{3,99},{4,5},{5,4},{6,7},{7,6},{8,104},{9,105... | collective-permute-start | bytes 4128776 | tf_op jit(solution)/shard_map/ppermute | solution.py:332
  53.9 20.2 %collective-permute-start.15 = (bf16[16,352,128]{2,1,0:T(8,128)(2,1)S(1)}, bf16[16,352,128]{2,1,0:T(8,128)(2,1)S(1)}, u32[]{:S(2)}, u32[]{:S(2)}) collective-permute-start(bf16[16,352,128]{2,1,0:T(8,128)(2,1)S(1)} %pad_maximum_fusion), channel_id=1, source_target_pairs={{0,24},{1,25},{2,26},{3,27},{4,36},{5,37},{6,38},{7,39},{8,16},{9,... | collective-permute-start | bytes 4325384 | tf_op jit(solution)/shard_map/ppermute | solution.py:332
  56.1 20.5 %collective-permute-start.19 = (bf16[16,336,128]{2,1,0:T(8,128)(2,1)S(1)}, bf16[16,336,128]{2,1,0:T(8,128)(2,1)S(1)}, u32[]{:S(2)}, u32[]{:S(2)}) collective-permute-start(bf16[16,336,128]{2,1,0:T(8,128)(2,1)S(1)} %pad_maximum_fusion.2), channel_id=1, source_target_pairs={{0,3},{1,2},{2,1},{3,0},{4,12},{5,13},{6,14},{7,15},{8,11},{9,10},... | collective-permute-start | bytes 4128776 | tf_op jit(solution)/shard_map/ppermute | solution.py:332
  73.5 33.4 %collective-permute-start.18 = (bf16[32,336,128]{2,1,0:T(8,128)(2,1)}, bf16[32,336,128]{2,1,0:T(8,128)(2,1)}, u32[]{:S(2)}, u32[]{:S(2)}) collective-permute-start(bf16[32,336,128]{2,1,0:T(8,128)(2,1)} %constant_dynamic-update-slice_fusion.2.lo1), channel_id=1, source_target_pairs={{0,8},{1,9},{2,10},{3,11},{4,100},{5,101},{6,102},{7,103},{8,0},{9... | collective-permute-start | bytes 8257544 | tf_op jit(solution)/shard_map/ppermute | solution.py:332
  75.4 35.8 %collective-permute-start.16 = (bf16[32,352,128]{2,1,0:T(8,128)(2,1)}, bf16[32,352,128]{2,1,0:T(8,128)(2,1)}, u32[]{:S(2)}, u32[]{:S(2)}) collective-permute-start(bf16[32,352,128]{2,1,0:T(8,128)(2,1)} %constant_dynamic-update-slice_fusion.lo0), channel_id=1, source_target_pairs={{0,1},{1,0},{2,3},{3,2},{4,28},{5,29},{6,30},{7,31},{8,9},{9,8},{1... | collective-permute-start | bytes 8650760 | tf_op jit(solution)/shard_map/ppermute | solution.py:332
  77.8 33.4 %collective-permute-start.20 = (bf16[32,336,128]{2,1,0:T(8,128)(2,1)}, bf16[32,336,128]{2,1,0:T(8,128)(2,1)}, u32[]{:S(2)}, u32[]{:S(2)}) collective-permute-start(bf16[32,336,128]{2,1,0:T(8,128)(2,1)} %constant_dynamic-update-slice_fusion.4.lo2), channel_id=1, source_target_pairs={{0,32},{1,33},{2,34},{3,35},{4,7},{5,6},{6,5},{7,4},{8,40},{9,41},... | collective-permute-start | bytes 8257544 | tf_op jit(solution)/shard_map/ppermute | solution.py:332
  143.9 34.2 %collective-permute-start.33 = (bf16[33,336,128]{2,1,0:T(8,128)(2,1)S(1)}, bf16[33,336,128]{2,1,0:T(8,128)(2,1)}, u32[]{:S(2)}, u32[]{:S(2)}) collective-permute-start(bf16[33,336,128]{2,1,0:T(8,128)(2,1)S(1)} %get-tuple-element.51), channel_id=1, source_target_pairs={{0,32},{1,33},{2,34},{3,35},{4,7},{5,6},{6,5},{7,4},{8,40},{9,41},... | collective-permute-start | bytes 8515592 | tf_op jit(solution)/shard_map/ppermute | solution.py:348
  153.7 41.6 %collective-permute-start.27 = (bf16[33,336,128]{2,1,0:T(8,128)(2,1)S(1)}, bf16[33,336,128]{2,1,0:T(8,128)(2,1)}, u32[]{:S(2)}, u32[]{:S(2)}) collective-permute-start(bf16[33,336,128]{2,1,0:T(8,128)(2,1)S(1)} %get-tuple-element.49), channel_id=1, source_target_pairs={{0,8},{1,9},{2,10},{3,11},{4,100},{5,101},{6,102},{7,103},{8,0},{9... | collective-permute-start | bytes 8515592 | tf_op jit(solution)/shard_map/ppermute | solution.py:348
  166.5 42.2 %collective-permute-start.21 = (bf16[33,352,128]{2,1,0:T(8,128)(2,1)S(1)}, bf16[33,352,128]{2,1,0:T(8,128)(2,1)S(1)}, u32[]{:S(2)}, u32[]{:S(2)}) collective-permute-start(bf16[33,352,128]{2,1,0:T(8,128)(2,1)S(1)} %get-tuple-element.47), channel_id=1, source_target_pairs={{0,1},{1,0},{2,3},{3,2},{4,28},{5,29},{6,30},{7,31},{8,9},{9,8},{1... | collective-permute-start | bytes 8921096 | tf_op jit(solution)/shard_map/ppermute | solution.py:348
  180.6 29.0 %collective-permute-start.34 = (bf16[16,336,128]{2,1,0:T(8,128)(2,1)S(1)}, bf16[16,336,128]{2,1,0:T(8,128)(2,1)S(1)}, u32[]{:S(2)}, u32[]{:S(2)}) collective-permute-start(bf16[16,336,128]{2,1,0:T(8,128)(2,1)S(1)} %get-tuple-element.57), channel_id=1, source_target_pairs={{0,3},{1,2},{2,1},{3,0},{4,12},{5,13},{6,14},{7,15},{8,11},{9,10},... | collective-permute-start | bytes 4128776 | tf_op jit(solution)/shard_map/ppermute | solution.py:348
  197.8 27.0 %collective-permute-start.28 = (bf16[16,336,128]{2,1,0:T(8,128)(2,1)S(1)}, bf16[16,336,128]{2,1,0:T(8,128)(2,1)S(1)}, u32[]{:S(2)}, u32[]{:S(2)}) collective-permute-start(bf16[16,336,128]{2,1,0:T(8,128)(2,1)S(1)} %get-tuple-element.55), channel_id=1, source_target_pairs={{0,96},{1,97},{2,98},{3,99},{4,5},{5,4},{6,7},{7,6},{8,104},{9,105... | collective-permute-start | bytes 4128776 | tf_op jit(solution)/shard_map/ppermute | solution.py:348
  209.5 27.7 %collective-permute-start.22 = (bf16[16,352,128]{2,1,0:T(8,128)(2,1)S(1)}, bf16[16,352,128]{2,1,0:T(8,128)(2,1)S(1)}, u32[]{:S(2)}, u32[]{:S(2)}) collective-permute-start(bf16[16,352,128]{2,1,0:T(8,128)(2,1)S(1)} %get-tuple-element.53), channel_id=1, source_target_pairs={{0,24},{1,25},{2,26},{3,27},{4,36},{5,37},{6,38},{7,39},{8,16},{9,... | collective-permute-start | bytes 4325384 | tf_op jit(solution)/shard_map/ppermute | solution.py:348
  210.8 33.5 %collective-permute-start.35 = (bf16[8,336,128]{2,1,0:T(8,128)(2,1)}, bf16[8,336,128]{2,1,0:T(8,128)(2,1)}, u32[]{:S(2)}, u32[]{:S(2)}) collective-permute-start(bf16[8,336,128]{2,1,0:T(8,128)(2,1)} %get-tuple-element.63), channel_id=1, source_target_pairs={{0,8},{1,9},{2,10},{3,11},{4,100},{5,101},{6,102},{7,103},{8,0},{9... | collective-permute-start | bytes 2064392 | tf_op jit(solution)/shard_map/ppermute | solution.py:348
  226.0 19.6 %collective-permute-start.29 = (bf16[8,336,128]{2,1,0:T(8,128)(2,1)}, bf16[8,336,128]{2,1,0:T(8,128)(2,1)}, u32[]{:S(2)}, u32[]{:S(2)}) collective-permute-start(bf16[8,336,128]{2,1,0:T(8,128)(2,1)} %get-tuple-element.61), channel_id=1, source_target_pairs={{0,1},{1,0},{2,3},{3,2},{4,28},{5,29},{6,30},{7,31},{8,9},{9,8},{1... | collective-permute-start | bytes 2064392 | tf_op jit(solution)/shard_map/ppermute | solution.py:348
  237.5 16.9 %collective-permute-start.23 = (bf16[8,352,128]{2,1,0:T(8,128)(2,1)S(1)}, bf16[8,352,128]{2,1,0:T(8,128)(2,1)S(1)}, u32[]{:S(2)}, u32[]{:S(2)}) collective-permute-start(bf16[8,352,128]{2,1,0:T(8,128)(2,1)S(1)} %get-tuple-element.59), channel_id=1, source_target_pairs={{0,32},{1,33},{2,34},{3,35},{4,7},{5,6},{6,5},{7,4},{8,40},{9,41},... | collective-permute-start | bytes 2162696 | tf_op jit(solution)/shard_map/ppermute | solution.py:348
  245.5 9.2 %collective-permute-start.36 = (bf16[4,336,128]{2,1,0:T(8,128)(2,1)S(1)}, bf16[4,336,128]{2,1,0:T(8,128)(2,1)S(1)}, u32[]{:S(2)}, u32[]{:S(2)}) collective-permute-start(bf16[4,336,128]{2,1,0:T(8,128)(2,1)S(1)} %get-tuple-element.73), channel_id=1, source_target_pairs={{0,96},{1,97},{2,98},{3,99},{4,5},{5,4},{6,7},{7,6},{8,104},{9,105... | collective-permute-start | bytes 1032200 | tf_op jit(solution)/shard_map/ppermute | solution.py:348
  246.9 9.0 %collective-permute-start.30 = (bf16[4,336,128]{2,1,0:T(8,128)(2,1)S(1)}, bf16[4,336,128]{2,1,0:T(8,128)(2,1)S(1)}, u32[]{:S(2)}, u32[]{:S(2)}) collective-permute-start(bf16[4,336,128]{2,1,0:T(8,128)(2,1)S(1)} %get-tuple-element.71), channel_id=1, source_target_pairs={{0,24},{1,25},{2,26},{3,27},{4,36},{5,37},{6,38},{7,39},{8,16},{9,... | collective-permute-start | bytes 1032200 | tf_op jit(solution)/shard_map/ppermute | solution.py:348
  254.6 9.8 %collective-permute-start.24 = (bf16[4,352,128]{2,1,0:T(8,128)(2,1)S(1)}, bf16[4,352,128]{2,1,0:T(8,128)(2,1)S(1)}, u32[]{:S(2)}, u32[]{:S(2)}) collective-permute-start(bf16[4,352,128]{2,1,0:T(8,128)(2,1)S(1)} %get-tuple-element.69), channel_id=1, source_target_pairs={{0,3},{1,2},{2,1},{3,0},{4,12},{5,13},{6,14},{7,15},{8,11},{9,10},... | collective-permute-start | bytes 1081352 | tf_op jit(solution)/shard_map/ppermute | solution.py:348
  254.8 5.5 %collective-permute-start.37 = (bf16[2,336,128]{2,1,0:T(8,128)(2,1)S(1)}, bf16[2,336,128]{2,1,0:T(8,128)(2,1)S(1)}, u32[]{:S(2)}, u32[]{:S(2)}) collective-permute-start(bf16[2,336,128]{2,1,0:T(8,128)(2,1)S(1)} %get-tuple-element.79), channel_id=1, source_target_pairs={{0,1},{1,0},{2,3},{3,2},{4,28},{5,29},{6,30},{7,31},{8,9},{9,8},{1... | collective-permute-start | bytes 516104 | tf_op jit(solution)/shard_map/ppermute | solution.py:348
  256.1 5.5 %collective-permute-start.31 = (bf16[2,336,128]{2,1,0:T(8,128)(2,1)S(1)}, bf16[2,336,128]{2,1,0:T(8,128)(2,1)S(1)}, u32[]{:S(2)}, u32[]{:S(2)}) collective-permute-start(bf16[2,336,128]{2,1,0:T(8,128)(2,1)S(1)} %get-tuple-element.77), channel_id=1, source_target_pairs={{0,32},{1,33},{2,34},{3,35},{4,7},{5,6},{6,5},{7,4},{8,40},{9,41},... | collective-permute-start | bytes 516104 | tf_op jit(solution)/shard_map/ppermute | solution.py:348
  260.3 15.7 %copy-start.1 = (bf16[128,1024]{1,0:T(8,128)(2,1)S(1)}, bf16[128,1024]{1,0:T(8,128)(2,1)}, u32[]{:S(2)}) copy-start(bf16[128,1024]{1,0:T(8,128)(2,1)} %param.13) | copy-start | bytes 786436
  260.4 5.8 %collective-permute-start.38 = (bf16[1,336,128]{2,1,0:T(8,128)(2,1)S(1)}, bf16[1,336,128]{2,1,0:T(8,128)(2,1)S(1)}, u32[]{:S(2)}, u32[]{:S(2)}) collective-permute-start(bf16[1,336,128]{2,1,0:T(8,128)(2,1)S(1)} %add_convert_fusion.26), channel_id=1, source_target_pairs={{0,24},{1,25},{2,26},{3,27},{4,36},{5,37},{6,38},{7,39},{8,16},{9,... | collective-permute-start | bytes 258056 | tf_op jit(solution)/shard_map/ppermute | solution.py:348
  261.6 8.7 %collective-permute-start.32 = (bf16[1,336,128]{2,1,0:T(8,128)(2,1)S(1)}, bf16[1,336,128]{2,1,0:T(8,128)(2,1)S(1)}, u32[]{:S(2)}, u32[]{:S(2)}) collective-permute-start(bf16[1,336,128]{2,1,0:T(8,128)(2,1)S(1)} %add_convert_fusion.28), channel_id=1, source_target_pairs={{0,3},{1,2},{2,1},{3,0},{4,12},{5,13},{6,14},{7,15},{8,11},{9,10},... | collective-permute-start | bytes 258056 | tf_op jit(solution)/shard_map/ppermute | solution.py:348
  264.5 15.8 %copy-start = (bf16[4096,256]{1,0:T(8,128)(2,1)S(1)}, bf16[4096,256]{1,0:T(8,128)(2,1)}, u32[]{:S(2)}) copy-start(bf16[4096,256]{1,0:T(8,128)(2,1)} %param.21) | copy-start | bytes 6291460
  264.6 5.6 %collective-permute-start.25 = (bf16[2,352,128]{2,1,0:T(8,128)(2,1)S(1)}, bf16[2,352,128]{2,1,0:T(8,128)(2,1)S(1)}, u32[]{:S(2)}, u32[]{:S(2)}) collective-permute-start(bf16[2,352,128]{2,1,0:T(8,128)(2,1)S(1)} %get-tuple-element.75), channel_id=1, source_target_pairs={{0,8},{1,9},{2,10},{3,11},{4,100},{5,101},{6,102},{7,103},{8,0},{9... | collective-permute-start | bytes 540680 | tf_op jit(solution)/shard_map/ppermute | solution.py:348
  270.2 5.8 %collective-permute-start.26 = (bf16[1,352,128]{2,1,0:T(8,128)(2,1)S(1)}, bf16[1,352,128]{2,1,0:T(8,128)(2,1)S(1)}, u32[]{:S(2)}, u32[]{:S(2)}) collective-permute-start(bf16[1,352,128]{2,1,0:T(8,128)(2,1)S(1)} %add_convert_fusion.24), channel_id=1, source_target_pairs={{0,96},{1,97},{2,98},{3,99},{4,5},{5,4},{6,7},{7,6},{8,104},{9,105... | collective-permute-start | bytes 270344 | tf_op jit(solution)/shard_map/ppermute | solution.py:348
  276.1 10.5 %collective-permute-start.41 = (bf16[128,1024]{1,0:T(8,128)(2,1)S(1)}, bf16[128,1024]{1,0:T(8,128)(2,1)S(1)}, u32[]{:S(2)}, u32[]{:S(2)}) collective-permute-start(bf16[128,1024]{1,0:T(8,128)(2,1)S(1)} %fusion.19), channel_id=1, source_target_pairs={{0,3},{1,2},{2,1},{3,0},{4,7},{5,6},{6,5},{7,4},{8,11},{9,10},{10,... | collective-permute-start | bytes 786440 | tf_op jit(solution)/shard_map/ppermute | solution.py:381
  276.7 9.9 %collective-permute-start.40 = (bf16[128,1024]{1,0:T(8,128)(2,1)S(1)}, bf16[128,1024]{1,0:T(8,128)(2,1)S(1)}, u32[]{:S(2)}, u32[]{:S(2)}) collective-permute-start(bf16[128,1024]{1,0:T(8,128)(2,1)S(1)} %fusion.19), channel_id=1, source_target_pairs={{0,2},{1,3},{2,0},{3,1},{4,6},{5,7},{6,4},{7,5},{8,10},{9,11},{10,... | collective-permute-start | bytes 786440 | tf_op jit(solution)/shard_map/ppermute | solution.py:381
  279.1 8.4 %collective-permute-start.39 = (bf16[128,1024]{1,0:T(8,128)(2,1)S(1)}, bf16[128,1024]{1,0:T(8,128)(2,1)S(1)}, u32[]{:S(2)}, u32[]{:S(2)}) collective-permute-start(bf16[128,1024]{1,0:T(8,128)(2,1)S(1)} %fusion.19), channel_id=1, source_target_pairs={{0,1},{1,0},{2,3},{3,2},{4,5},{5,4},{6,7},{7,6},{8,9},{9,8},{10,11... | collective-permute-start | bytes 786440 | tf_op jit(solution)/shard_map/ppermute | solution.py:381
  (7 other events, 34.3 us)

commit v2 on v1

--- a/solution.py
+++ b/solution.py
@@ -333,7 +333,7 @@
         if stage == STAGES - 1:
             return list(zip(held, got)), far, routes
         held = [jnp.concatenate([h, g], axis=0) for h, g in zip(held, got)]
-        if 1 <= stage <= 2:
+        if stage == 2:
             held, far, weights = lax.optimization_barrier((held, far, weights))
         if stage == 3:
             held, far, routes = lax.optimization_barrier((held, far, routes))

time: 291 us -> 288 us (0.990)
  Pallas kernels: 51.4 us -> 47.7 us
  transfers between devices with their start and end apart: 43 -> 43, of which waited for: 27 -> 22; matrix products, arithmetic and copies ran while one was open for 13% -> 13% of each run, Pallas kernels for 6% -> 6%
where the time goes in v2:
time: 288 us; the launch traced here: 287 us
  waiting for transfers between devices  141 us (49%)
  starting transfers between devices  56.1 us (19%)
  Pallas kernels  47.7 us (17%)
  other arithmetic  22.7 us (8%)
  local copies, waits for them, and re-layouts  16.8 us (6%)
    ppermute x18, waiting for transfers between devices, collect(): got = lax.ppermute(high, AXES, stage_pairs(part, stage))  79.4 us
    ppermute x18, waiting for transfers between devices, spread(): lax.ppermute(held[p], AXES, stage_pairs(p, stage))  50.5 us
    pallas_call x3, Pallas kernels, find_sums(): pl.pallas_call(functools.partial(down_kernel, part), in_specs=[smem, smem...  25.8 us
    ppermute x18, starting transfers between devices, collect(): got = lax.ppermute(high, AXES, stage_pairs(part, stage))  24.9 us
    pallas_call x1, Pallas kernels, find_hidden(): pl.pallas_call(hidden_kernel, in_specs=[smem, smem, vmem, vmem] + [anywhe...  21.9 us
    ppermute x18, starting transfers between devices, spread(): lax.ppermute(held[p], AXES, stage_pairs(p, stage))  19 us
    convert_element_type x15, other arithmetic, add(): return (a.astype(jnp.float32) + b.astype(jnp.float32)).astype(jnp.bfloat16)  11.6 us
    all_to_all x1, starting transfers between devices, on_device(): lax.all_to_all(routes, ('y', 'z'), split_axis=0, concat_axis=0, tiled=True)  7.38 us
  transfers between devices with their start and end apart: 43, of which 22 were waited for; matrix products, arithmetic and copies ran while one was open for 13% of the time, Pallas kernels for 6%

profile of v2, /device:TPU:0, one launch (start us, length us, event | category | flops | bytes accessed | tf_op | source)
XLA Modules:
  0.0 286.8 jit_solution(13877693325782378194)
XLA Ops:
  2.2 2.9 %collective-permute-start.3 = (bf16[1,336,128]{2,1,0:T(8,128)(2,1)S(1)}, bf16[1,336,128]{2,1,0:T(8,128)(2,1)S(1)}, u32[]{:S(2)}, u32[]{:S(2)}) collective-permute-start(bf16[1,336,128]{2,1,0:T(8,128)(2,1)S(1)} %get-tuple-element.69), channel_id=1, source_target_pairs={{0,3},{1,2},{2,1},{3,0},{4,12},{5,13},{6,14},{7,15},{8,11},{9,10},... | collective-permute-start | bytes 258056 | tf_op jit(solution)/shard_map/ppermute | solution.py:332
  5.2 3.0 %collective-permute-start = (bf16[1,352,128]{2,1,0:T(8,128)(2,1)S(1)}, bf16[1,352,128]{2,1,0:T(8,128)(2,1)S(1)}, u32[]{:S(2)}, u32[]{:S(2)}) collective-permute-start(bf16[1,352,128]{2,1,0:T(8,128)(2,1)S(1)} %slice_bitcast_fusion), channel_id=1, source_target_pairs={{0,96},{1,97},{2,98},{3,99},{4,5},{5,4},{6,7},{7,6},{8,104},{9,105... | collective-permute-start | bytes 270344 | tf_op jit(solution)/shard_map/ppermute | solution.py:332
  8.2 4.0 %collective-permute-start.6 = (bf16[1,336,128]{2,1,0:T(8,128)(2,1)S(1)}, bf16[1,336,128]{2,1,0:T(8,128)(2,1)S(1)}, u32[]{:S(2)}, u32[]{:S(2)}) collective-permute-start(bf16[1,336,128]{2,1,0:T(8,128)(2,1)S(1)} %get-tuple-element.68), channel_id=1, source_target_pairs={{0,24},{1,25},{2,26},{3,27},{4,36},{5,37},{6,38},{7,39},{8,16},{9,... | collective-permute-start | bytes 258056 | tf_op jit(solution)/shard_map/ppermute | solution.py:332
  12.5 3.0 %collective-permute-done.6 = bf16[1,336,128]{2,1,0:T(8,128)(2,1)S(1)} collective-permute-done((bf16[1,336,128]{2,1,0:T(8,128)(2,1)S(1)}, bf16[1,336,128]{2,1,0:T(8,128)(2,1)S(1)}, u32[]{:S(2)}, u32[]{:S(2)}) %collective-permute-start.6) | collective-permute-done | bytes 86048 | tf_op jit(solution)/shard_map/ppermute | solution.py:332
  16.0 1.7 collective-permute-done.4
  17.8 1.6 collective-permute-start.5
  19.4 3.4 %collective-permute-done.7 = bf16[2,336,128]{2,1,0:T(8,128)(2,1)S(1)} collective-permute-done((bf16[2,336,128]{2,1,0:T(8,128)(2,1)S(1)}, bf16[2,336,128]{2,1,0:T(8,128)(2,1)S(1)}, u32[]{:S(2)}, u32[]{:S(2)}) %collective-permute-start.7) | collective-permute-done | bytes 172064 | tf_op jit(solution)/shard_map/ppermute | solution.py:332
  23.8 2.5 collective-permute-done.5
  26.4 5.0 %collective-permute-done.8 = bf16[4,336,128]{2,1,0:T(8,128)(2,1)S(1)} collective-permute-done((bf16[4,336,128]{2,1,0:T(8,128)(2,1)S(1)}, bf16[4,336,128]{2,1,0:T(8,128)(2,1)S(1)}, u32[]{:S(2)}, u32[]{:S(2)}) %collective-permute-start.8) | collective-permute-done | bytes 344096 | tf_op jit(solution)/shard_map/ppermute | solution.py:332
  33.1 1.4 select_reduce_fusion.1
  34.5 1.9 copy-done.10
  36.4 7.4 %all-to-all-start = ((f32[16,4,128]{2,1,0:T(4,128)}), f32[16,4,128]{2,1,0:T(4,128)}, u32[]{:S(2)}, u32[]{:S(2)}) async-start(f32[16,4,128]{2,1,0:T(4,128)} %bitcast.8), calls=%async_computation | async-start | bytes 65536 | tf_op jit(solution)/shard_map/all_to_all | solution.py:368
  47.5 4.0 %all-to-all-done = f32[16,4,128]{2,1,0:T(4,128)} async-done(((f32[16,4,128]{2,1,0:T(4,128)}), f32[16,4,128]{2,1,0:T(4,128)}, u32[]{:S(2)}, u32[]{:S(2)}) %all-to-all-start) | async-done | bytes 32800 | tf_op jit(solution)/shard_map/all_to_all | solution.py:368
  52.5 1.3 collective-permute-start.15
  54.3 2.5 constant_dynamic-update-slice_fusion.3
  59.3 11.9 %collective-permute-done.17 = bf16[16,336,128]{2,1,0:T(8,128)(2,1)S(1)} collective-permute-done((bf16[16,336,128]{2,1,0:T(8,128)(2,1)}, bf16[16,336,128]{2,1,0:T(8,128)(2,1)S(1)}, u32[]{:S(2)}, u32[]{:S(2)}) %collective-permute-start.17) | collective-permute-done | bytes 1376288 | tf_op jit(solution)/shard_map/ppermute | solution.py:332
  74.1 1.3 collective-permute-start.16
  79.7 1.9 copy.48
  81.6 1.9 and_convert_fusion
  85.4 1.9 fusion.30.put
  87.3 18.5 %collective-permute-done.18.hi1 = bf16[32,336,128]{2,1,0:T(8,128)(2,1)} collective-permute-done((bf16[32,336,128]{2,1,0:T(8,128)(2,1)}, bf16[32,336,128]{2,1,0:T(8,128)(2,1)}, u32[]{:S(2)}, u32[]{:S(2)}) %collective-permute-start.18) | collective-permute-done | bytes 2752544 | tf_op jit(solution)/shard_map/ppermute | solution.py:332
  105.8 4.2 %collective-permute-done.20.hi2 = bf16[32,336,128]{2,1,0:T(8,128)(2,1)} collective-permute-done((bf16[32,336,128]{2,1,0:T(8,128)(2,1)}, bf16[32,336,128]{2,1,0:T(8,128)(2,1)}, u32[]{:S(2)}, u32[]{:S(2)}) %collective-permute-start.20) | collective-permute-done | bytes 2752544 | tf_op jit(solution)/shard_map/ppermute | solution.py:332
  110.0 21.9 %hidden.1 = bf16[4,512,384]{2,1,0:T(8,128)(2,1)S(1)} custom-call(s32[192]{0:T(256)S(1)} %bitcast.53, s32[4]{0:T(128)S(1)} %fusion.23.groups, bf16[8,256,256]{2,1,0:T(8,128)(2,1)S(1)} %copy.53.pick, f32[4,512,1]{2,1,0:T(8,128)S(1)} %reshape.72.weight, bf16[32,352,128]{2,1,0:T(8,128)(2,1)} %constant_dynamic-update-slice_fusion.lo0, ...), custom_call_target="tpu_custom_call" | custom-call | flops 17179869184 | bytes 104857600 | tf_op jit(solution)/shard_map/hidden/pallas_call | solution.py:186
  131.9 8.4 %sums.5 = (bf16[33,336,128]{2,1,0:T(8,128)(2,1)S(1)}, bf16[33,336,128]{2,1,0:T(8,128)(2,1)S(1)}) custom-call(s32[4]{0:T(128)S(1)} %fusion.23.groups, s32[192]{0:T(256)S(1)} %bitcast.54, bf16[8,256,256]{2,1,0:T(8,128)(2,1)S(1)} %fusion.30.put, bf16[4,512,384]{2,1,0:T(8,128)(2,1)S(1)} %hidden.1, bf16[2,384,4096]{2,1,0:T(8,128)(2,1)} %d_own.5, ...), custom_call_target="tpu_custom_call" | custom-call | flops 4026531840 | bytes 41943040 | tf_op jit(solution)/shard_map/sums/pallas_call | solution.py:280
  140.4 1.3 collective-permute-start.33
  141.7 8.9 %sums.4 = (bf16[33,336,128]{2,1,0:T(8,128)(2,1)S(1)}, bf16[33,336,128]{2,1,0:T(8,128)(2,1)S(1)}) custom-call(s32[4]{0:T(128)S(1)} %fusion.23.groups, s32[192]{0:T(256)S(1)} %bitcast.55, bf16[8,256,256]{2,1,0:T(8,128)(2,1)S(1)} %fusion.30.put, bf16[4,512,384]{2,1,0:T(8,128)(2,1)S(1)} %hidden.1, bf16[2,384,4096]{2,1,0:T(8,128)(2,1)} %d_own.5, ...), custom_call_target="tpu_custom_call" | custom-call | flops 5368709120 | bytes 41943040 | tf_op jit(solution)/shard_map/sums/pallas_call | solution.py:280
  150.6 5.7 %collective-permute-start.27 = (bf16[33,336,128]{2,1,0:T(8,128)(2,1)S(1)}, bf16[33,336,128]{2,1,0:T(8,128)(2,1)}, u32[]{:S(2)}, u32[]{:S(2)}) collective-permute-start(bf16[33,336,128]{2,1,0:T(8,128)(2,1)S(1)} %get-tuple-element.37), channel_id=1, source_target_pairs={{0,8},{1,9},{2,10},{3,11},{4,100},{5,101},{6,102},{7,103},{8,0},{9... | collective-permute-start | bytes 8515592 | tf_op jit(solution)/shard_map/ppermute | solution.py:348
  156.3 8.4 %sums.3 = (bf16[33,352,128]{2,1,0:T(8,128)(2,1)S(1)}, bf16[33,352,128]{2,1,0:T(8,128)(2,1)S(1)}) custom-call(s32[4]{0:T(128)S(1)} %fusion.23.groups, s32[192]{0:T(256)S(1)} %bitcast.56, bf16[8,256,256]{2,1,0:T(8,128)(2,1)S(1)} %fusion.30.put, bf16[4,512,384]{2,1,0:T(8,128)(2,1)S(1)} %hidden.1, bf16[2,384,4096]{2,1,0:T(8,128)(2,1)} %d_own.5, ...), custom_call_target="tpu_custom_call" | custom-call | flops 4026531840 | bytes 41943040 | tf_op jit(solution)/shard_map/sums/pallas_call | solution.py:280
  165.5 9.0 %collective-permute-done.33 = bf16[33,336,128]{2,1,0:T(8,128)(2,1)} collective-permute-done((bf16[33,336,128]{2,1,0:T(8,128)(2,1)S(1)}, bf16[33,336,128]{2,1,0:T(8,128)(2,1)}, u32[]{:S(2)}, u32[]{:S(2)}) %collective-permute-start.33) | collective-permute-done | bytes 2838560 | tf_op jit(solution)/shard_map/ppermute | solution.py:348
  174.5 2.5 add_convert_fusion.3
  177.8 20.1 %collective-permute-done.27 = bf16[33,336,128]{2,1,0:T(8,128)(2,1)} collective-permute-done((bf16[33,336,128]{2,1,0:T(8,128)(2,1)S(1)}, bf16[33,336,128]{2,1,0:T(8,128)(2,1)}, u32[]{:S(2)}, u32[]{:S(2)}) %collective-permute-start.27) | collective-permute-done | bytes 2838560 | tf_op jit(solution)/shard_map/ppermute | solution.py:348
  197.8 2.5 add_convert_fusion.5
  201.2 8.8 %collective-permute-done.21 = bf16[33,352,128]{2,1,0:T(8,128)(2,1)S(1)} collective-permute-done((bf16[33,352,128]{2,1,0:T(8,128)(2,1)S(1)}, bf16[33,352,128]{2,1,0:T(8,128)(2,1)S(1)}, u32[]{:S(2)}, u32[]{:S(2)}) %collective-permute-start.21) | collective-permute-done | bytes 2973728 | tf_op jit(solution)/shard_map/ppermute | solution.py:348
  212.1 1.8 collective-permute-start.35
  213.8 13.4 %collective-permute-done.28 = bf16[16,336,128]{2,1,0:T(8,128)(2,1)S(1)} collective-permute-done((bf16[16,336,128]{2,1,0:T(8,128)(2,1)S(1)}, bf16[16,336,128]{2,1,0:T(8,128)(2,1)S(1)}, u32[]{:S(2)}, u32[]{:S(2)}) %collective-permute-start.28) | collective-permute-done | bytes 1376288 | tf_op jit(solution)/shard_map/ppermute | solution.py:348
  228.5 2.7 collective-permute-start.29
  231.2 7.2 %collective-permute-done.22 = bf16[16,352,128]{2,1,0:T(8,128)(2,1)S(1)} collective-permute-done((bf16[16,352,128]{2,1,0:T(8,128)(2,1)S(1)}, bf16[16,352,128]{2,1,0:T(8,128)(2,1)S(1)}, u32[]{:S(2)}, u32[]{:S(2)}) %collective-permute-start.22) | collective-permute-done | bytes 1441824 | tf_op jit(solution)/shard_map/ppermute | solution.py:348
  238.8 2.0 collective-permute-start.23
  244.5 7.3 %collective-permute-done.23 = bf16[8,352,128]{2,1,0:T(8,128)(2,1)S(1)} collective-permute-done((bf16[8,352,128]{2,1,0:T(8,128)(2,1)S(1)}, bf16[8,352,128]{2,1,0:T(8,128)(2,1)S(1)}, u32[]{:S(2)}, u32[]{:S(2)}) %collective-permute-start.23) | collective-permute-done | bytes 720928 | tf_op jit(solution)/shard_map/ppermute | solution.py:348
  253.0 1.8 collective-permute-start.31
  254.9 3.3 %collective-permute-done.37 = bf16[2,336,128]{2,1,0:T(8,128)(2,1)S(1)} collective-permute-done((bf16[2,336,128]{2,1,0:T(8,128)(2,1)S(1)}, bf16[2,336,128]{2,1,0:T(8,128)(2,1)S(1)}, u32[]{:S(2)}, u32[]{:S(2)}) %collective-permute-start.37) | collective-permute-done | bytes 172064 | tf_op jit(solution)/shard_map/ppermute | solution.py:348
  258.6 3.8 %collective-permute-start.32 = (bf16[1,336,128]{2,1,0:T(8,128)(2,1)S(1)}, bf16[1,336,128]{2,1,0:T(8,128)(2,1)S(1)}, u32[]{:S(2)}, u32[]{:S(2)}) collective-permute-start(bf16[1,336,128]{2,1,0:T(8,128)(2,1)S(1)} %add_convert_fusion.28), channel_id=1, source_target_pairs={{0,3},{1,2},{2,1},{3,0},{4,12},{5,13},{6,14},{7,15},{8,11},{9,10},... | collective-permute-start | bytes 258056 | tf_op jit(solution)/shard_map/ppermute | solution.py:348
  262.5 1.4 collective-permute-done.38
  264.0 4.1 %collective-permute-done.25 = bf16[2,352,128]{2,1,0:T(8,128)(2,1)S(1)} collective-permute-done((bf16[2,352,128]{2,1,0:T(8,128)(2,1)S(1)}, bf16[2,352,128]{2,1,0:T(8,128)(2,1)S(1)}, u32[]{:S(2)}, u32[]{:S(2)}) %collective-permute-start.25) | collective-permute-done | bytes 180256 | tf_op jit(solution)/shard_map/ppermute | solution.py:348
  268.9 4.9 %collective-permute-done.26 = bf16[1,352,128]{2,1,0:T(8,128)(2,1)S(1)} collective-permute-done((bf16[1,352,128]{2,1,0:T(8,128)(2,1)S(1)}, bf16[1,352,128]{2,1,0:T(8,128)(2,1)S(1)}, u32[]{:S(2)}, u32[]{:S(2)}) %collective-permute-start.26) | collective-permute-done | bytes 90144 | tf_op jit(solution)/shard_map/ppermute | solution.py:348
  274.1 2.3 collective-permute-start.40
  276.4 1.8 collective-permute-start.39
  278.4 6.2 %collective-permute-done.41 = bf16[128,1024]{1,0:T(8,128)(2,1)S(1)} collective-permute-done((bf16[128,1024]{1,0:T(8,128)(2,1)S(1)}, bf16[128,1024]{1,0:T(8,128)(2,1)S(1)}, u32[]{:S(2)}, u32[]{:S(2)}) %collective-permute-start.41) | collective-permute-done | bytes 262176 | tf_op jit(solution)/shard_map/ppermute | solution.py:381
  (140 shorter events, 37.0 us)
Async XLA Ops:
  0.6 31.2 %collective-permute-start.9 = (bf16[2,4096,384]{2,1,0:T(8,128)(2,1)}, bf16[2,4096,384]{2,1,0:T(8,128)(2,1)S(1)}, u32[]{:S(2)}, u32[]{:S(2)}) collective-permute-start(bf16[2,4096,384]{2,1,0:T(8,128)(2,1)} %g_own.1), channel_id=1, source_target_pairs={{0,4},{1,5},{2,6},{3,7},{4,0},{5,1},{6,2},{7,3},{8,12},{9,13},{10,... | collective-permute-start | bytes 18874376 | tf_op jit(solution)/shard_map/ppermute | solution.py:331
  0.7 31.1 %collective-permute-start.10 = (bf16[2,4096,384]{2,1,0:T(8,128)(2,1)}, bf16[2,4096,384]{2,1,0:T(8,128)(2,1)S(1)}, u32[]{:S(2)}, u32[]{:S(2)}) collective-permute-start(bf16[2,4096,384]{2,1,0:T(8,128)(2,1)} %u_own.1), channel_id=1, source_target_pairs={{0,4},{1,5},{2,6},{3,7},{4,0},{5,1},{6,2},{7,3},{8,12},{9,13},{10,... | collective-permute-start | bytes 18874376 | tf_op jit(solution)/shard_map/ppermute | solution.py:331
  2.2 10.0 %collective-permute-start.3 = (bf16[1,336,128]{2,1,0:T(8,128)(2,1)S(1)}, bf16[1,336,128]{2,1,0:T(8,128)(2,1)S(1)}, u32[]{:S(2)}, u32[]{:S(2)}) collective-permute-start(bf16[1,336,128]{2,1,0:T(8,128)(2,1)S(1)} %get-tuple-element.69), channel_id=1, source_target_pairs={{0,3},{1,2},{2,1},{3,0},{4,12},{5,13},{6,14},{7,15},{8,11},{9,10},... | collective-permute-start | bytes 258056 | tf_op jit(solution)/shard_map/ppermute | solution.py:332
  5.2 10.8 %collective-permute-start = (bf16[1,352,128]{2,1,0:T(8,128)(2,1)S(1)}, bf16[1,352,128]{2,1,0:T(8,128)(2,1)S(1)}, u32[]{:S(2)}, u32[]{:S(2)}) collective-permute-start(bf16[1,352,128]{2,1,0:T(8,128)(2,1)S(1)} %slice_bitcast_fusion), channel_id=1, source_target_pairs={{0,96},{1,97},{2,98},{3,99},{4,5},{5,4},{6,7},{7,6},{8,104},{9,105... | collective-permute-start | bytes 270344 | tf_op jit(solution)/shard_map/ppermute | solution.py:332
  8.2 7.3 %collective-permute-start.6 = (bf16[1,336,128]{2,1,0:T(8,128)(2,1)S(1)}, bf16[1,336,128]{2,1,0:T(8,128)(2,1)S(1)}, u32[]{:S(2)}, u32[]{:S(2)}) collective-permute-start(bf16[1,336,128]{2,1,0:T(8,128)(2,1)S(1)} %get-tuple-element.68), channel_id=1, source_target_pairs={{0,24},{1,25},{2,26},{3,27},{4,36},{5,37},{6,38},{7,39},{8,16},{9,... | collective-permute-start | bytes 258056 | tf_op jit(solution)/shard_map/ppermute | solution.py:332
  12.2 5.5 %collective-permute-start.4 = (bf16[2,336,128]{2,1,0:T(8,128)(2,1)S(1)}, bf16[2,336,128]{2,1,0:T(8,128)(2,1)S(1)}, u32[]{:S(2)}, u32[]{:S(2)}) collective-permute-start(bf16[2,336,128]{2,1,0:T(8,128)(2,1)S(1)} %pad_maximum_fusion.13), channel_id=1, source_target_pairs={{0,32},{1,33},{2,34},{3,35},{4,7},{5,6},{6,5},{7,4},{8,40},{9,41},... | collective-permute-start | bytes 516104 | tf_op jit(solution)/shard_map/ppermute | solution.py:332
  15.5 7.3 %collective-permute-start.7 = (bf16[2,336,128]{2,1,0:T(8,128)(2,1)S(1)}, bf16[2,336,128]{2,1,0:T(8,128)(2,1)S(1)}, u32[]{:S(2)}, u32[]{:S(2)}) collective-permute-start(bf16[2,336,128]{2,1,0:T(8,128)(2,1)S(1)} %pad_maximum_fusion.14), channel_id=1, source_target_pairs={{0,1},{1,0},{2,3},{3,2},{4,28},{5,29},{6,30},{7,31},{8,9},{9,8},{1... | collective-permute-start | bytes 516104 | tf_op jit(solution)/shard_map/ppermute | solution.py:332
  16.0 7.0 %collective-permute-start.1 = (bf16[2,352,128]{2,1,0:T(8,128)(2,1)S(1)}, bf16[2,352,128]{2,1,0:T(8,128)(2,1)S(1)}, u32[]{:S(2)}, u32[]{:S(2)}) collective-permute-start(bf16[2,352,128]{2,1,0:T(8,128)(2,1)S(1)} %pad_maximum_fusion.11), channel_id=1, source_target_pairs={{0,8},{1,9},{2,10},{3,11},{4,100},{5,101},{6,102},{7,103},{8,0},{9... | collective-permute-start | bytes 540680 | tf_op jit(solution)/shard_map/ppermute | solution.py:332
  17.8 8.5 %collective-permute-start.5 = (bf16[4,336,128]{2,1,0:T(8,128)(2,1)S(1)}, bf16[4,336,128]{2,1,0:T(8,128)(2,1)S(1)}, u32[]{:S(2)}, u32[]{:S(2)}) collective-permute-start(bf16[4,336,128]{2,1,0:T(8,128)(2,1)S(1)} %pad_maximum_fusion.9), channel_id=1, source_target_pairs={{0,24},{1,25},{2,26},{3,27},{4,36},{5,37},{6,38},{7,39},{8,16},{9,... | collective-permute-start | bytes 1032200 | tf_op jit(solution)/shard_map/ppermute | solution.py:332
  22.8 8.5 %collective-permute-start.8 = (bf16[4,336,128]{2,1,0:T(8,128)(2,1)S(1)}, bf16[4,336,128]{2,1,0:T(8,128)(2,1)S(1)}, u32[]{:S(2)}, u32[]{:S(2)}) collective-permute-start(bf16[4,336,128]{2,1,0:T(8,128)(2,1)S(1)} %pad_maximum_fusion.10), channel_id=1, source_target_pairs={{0,96},{1,97},{2,98},{3,99},{4,5},{5,4},{6,7},{7,6},{8,104},{9,105... | collective-permute-start | bytes 1032200 | tf_op jit(solution)/shard_map/ppermute | solution.py:332
  23.0 10.1 %copy-start.6 = (f32[128,8]{0,1:T(8,128)S(1)}, f32[128,8]{0,1:T(8,128)}, u32[]{:S(2)}) copy-start(f32[128,8]{0,1:T(8,128)} %param.16) | copy-start | bytes 12292
  23.0 10.1 %copy-start.7 = (s32[128,8]{0,1:T(8,128)S(1)}, s32[128,8]{0,1:T(8,128)}, u32[]{:S(2)}) copy-start(s32[128,8]{0,1:T(8,128)} %param.15) | copy-start | bytes 12292
  23.0 8.7 %collective-permute-start.2 = (bf16[4,352,128]{2,1,0:T(8,128)(2,1)S(1)}, bf16[4,352,128]{2,1,0:T(8,128)(2,1)S(1)}, u32[]{:S(2)}, u32[]{:S(2)}) collective-permute-start(bf16[4,352,128]{2,1,0:T(8,128)(2,1)S(1)} %pad_maximum_fusion.8), channel_id=1, source_target_pairs={{0,3},{1,2},{2,1},{3,0},{4,12},{5,13},{6,14},{7,15},{8,11},{9,10},... | collective-permute-start | bytes 1081352 | tf_op jit(solution)/shard_map/ppermute | solution.py:332
  31.8 19.6 %collective-permute-start.14 = (bf16[2,384,4096]{2,1,0:T(8,128)(2,1)}, bf16[2,384,4096]{2,1,0:T(8,128)(2,1)}, u32[]{:S(2)}, u32[]{:S(2)}) collective-permute-start(bf16[2,384,4096]{2,1,0:T(8,128)(2,1)} %d_own.5), channel_id=1, source_target_pairs={{0,4},{1,5},{2,6},{3,7},{4,0},{5,1},{6,2},{7,3},{8,12},{9,13},{10,... | collective-permute-start | bytes 18874376 | tf_op jit(solution)/shard_map/ppermute | solution.py:331
  31.9 11.9 %collective-permute-start.12 = (bf16[8,336,128]{2,1,0:T(8,128)(2,1)S(1)}, bf16[8,336,128]{2,1,0:T(8,128)(2,1)S(1)}, u32[]{:S(2)}, u32[]{:S(2)}) collective-permute-start(bf16[8,336,128]{2,1,0:T(8,128)(2,1)S(1)} %pad_maximum_fusion.5), channel_id=1, source_target_pairs={{0,1},{1,0},{2,3},{3,2},{4,28},{5,29},{6,30},{7,31},{8,9},{9,8},{1... | collective-permute-start | bytes 2064392 | tf_op jit(solution)/shard_map/ppermute | solution.py:332
  33.0 12.0 %collective-permute-start.13 = (bf16[8,336,128]{2,1,0:T(8,128)(2,1)S(1)}, bf16[8,336,128]{2,1,0:T(8,128)(2,1)}, u32[]{:S(2)}, u32[]{:S(2)}) collective-permute-start(bf16[8,336,128]{2,1,0:T(8,128)(2,1)S(1)} %pad_maximum_fusion.6), channel_id=1, source_target_pairs={{0,8},{1,9},{2,10},{3,11},{4,100},{5,101},{6,102},{7,103},{8,0},{9... | collective-permute-start | bytes 2064392 | tf_op jit(solution)/shard_map/ppermute | solution.py:332
  33.0 13.2 %collective-permute-start.11 = (bf16[8,352,128]{2,1,0:T(8,128)(2,1)S(1)}, bf16[8,352,128]{2,1,0:T(8,128)(2,1)}, u32[]{:S(2)}, u32[]{:S(2)}) collective-permute-start(bf16[8,352,128]{2,1,0:T(8,128)(2,1)S(1)} %pad_maximum_fusion.4), channel_id=1, source_target_pairs={{0,32},{1,33},{2,34},{3,35},{4,7},{5,6},{6,5},{7,4},{8,40},{9,41},... | collective-permute-start | bytes 2162696 | tf_op jit(solution)/shard_map/ppermute | solution.py:332
  36.4 15.1 %all-to-all-start = ((f32[16,4,128]{2,1,0:T(4,128)}), f32[16,4,128]{2,1,0:T(4,128)}, u32[]{:S(2)}, u32[]{:S(2)}) async-start(f32[16,4,128]{2,1,0:T(4,128)} %bitcast.8), calls=%async_computation | async-start | bytes 65536 | tf_op jit(solution)/shard_map/all_to_all | solution.py:368
  51.5 19.7 %collective-permute-start.17 = (bf16[16,336,128]{2,1,0:T(8,128)(2,1)}, bf16[16,336,128]{2,1,0:T(8,128)(2,1)S(1)}, u32[]{:S(2)}, u32[]{:S(2)}) collective-permute-start(bf16[16,336,128]{2,1,0:T(8,128)(2,1)} %pad_maximum_fusion.1), channel_id=1, source_target_pairs={{0,96},{1,97},{2,98},{3,99},{4,5},{5,4},{6,7},{7,6},{8,104},{9,105... | collective-permute-start | bytes 4128776 | tf_op jit(solution)/shard_map/ppermute | solution.py:332
  52.5 20.3 %collective-permute-start.15 = (bf16[16,352,128]{2,1,0:T(8,128)(2,1)S(1)}, bf16[16,352,128]{2,1,0:T(8,128)(2,1)S(1)}, u32[]{:S(2)}, u32[]{:S(2)}) collective-permute-start(bf16[16,352,128]{2,1,0:T(8,128)(2,1)S(1)} %pad_maximum_fusion), channel_id=1, source_target_pairs={{0,24},{1,25},{2,26},{3,27},{4,36},{5,37},{6,38},{7,39},{8,16},{9,... | collective-permute-start | bytes 4325384 | tf_op jit(solution)/shard_map/ppermute | solution.py:332
  53.8 21.6 %collective-permute-start.19 = (bf16[16,336,128]{2,1,0:T(8,128)(2,1)S(1)}, bf16[16,336,128]{2,1,0:T(8,128)(2,1)S(1)}, u32[]{:S(2)}, u32[]{:S(2)}) collective-permute-start(bf16[16,336,128]{2,1,0:T(8,128)(2,1)S(1)} %pad_maximum_fusion.2), channel_id=1, source_target_pairs={{0,3},{1,2},{2,1},{3,0},{4,12},{5,13},{6,14},{7,15},{8,11},{9,10},... | collective-permute-start | bytes 4128776 | tf_op jit(solution)/shard_map/ppermute | solution.py:332
  72.4 33.4 %collective-permute-start.18 = (bf16[32,336,128]{2,1,0:T(8,128)(2,1)}, bf16[32,336,128]{2,1,0:T(8,128)(2,1)}, u32[]{:S(2)}, u32[]{:S(2)}) collective-permute-start(bf16[32,336,128]{2,1,0:T(8,128)(2,1)} %constant_dynamic-update-slice_fusion.2.lo1), channel_id=1, source_target_pairs={{0,8},{1,9},{2,10},{3,11},{4,100},{5,101},{6,102},{7,103},{8,0},{9... | collective-permute-start | bytes 8257544 | tf_op jit(solution)/shard_map/ppermute | solution.py:332
  74.1 35.9 %collective-permute-start.16 = (bf16[32,352,128]{2,1,0:T(8,128)(2,1)}, bf16[32,352,128]{2,1,0:T(8,128)(2,1)}, u32[]{:S(2)}, u32[]{:S(2)}) collective-permute-start(bf16[32,352,128]{2,1,0:T(8,128)(2,1)} %constant_dynamic-update-slice_fusion.lo0), channel_id=1, source_target_pairs={{0,1},{1,0},{2,3},{3,2},{4,28},{5,29},{6,30},{7,31},{8,9},{9,8},{1... | collective-permute-start | bytes 8650760 | tf_op jit(solution)/shard_map/ppermute | solution.py:332
  76.6 33.4 %collective-permute-start.20 = (bf16[32,336,128]{2,1,0:T(8,128)(2,1)}, bf16[32,336,128]{2,1,0:T(8,128)(2,1)}, u32[]{:S(2)}, u32[]{:S(2)}) collective-permute-start(bf16[32,336,128]{2,1,0:T(8,128)(2,1)} %constant_dynamic-update-slice_fusion.4.lo2), channel_id=1, source_target_pairs={{0,32},{1,33},{2,34},{3,35},{4,7},{5,6},{6,5},{7,4},{8,40},{9,41},... | collective-permute-start | bytes 8257544 | tf_op jit(solution)/shard_map/ppermute | solution.py:332
  140.4 34.2 %collective-permute-start.33 = (bf16[33,336,128]{2,1,0:T(8,128)(2,1)S(1)}, bf16[33,336,128]{2,1,0:T(8,128)(2,1)}, u32[]{:S(2)}, u32[]{:S(2)}) collective-permute-start(bf16[33,336,128]{2,1,0:T(8,128)(2,1)S(1)} %get-tuple-element.39), channel_id=1, source_target_pairs={{0,32},{1,33},{2,34},{3,35},{4,7},{5,6},{6,5},{7,4},{8,40},{9,41},... | collective-permute-start | bytes 8515592 | tf_op jit(solution)/shard_map/ppermute | solution.py:348
  150.6 47.2 %collective-permute-start.27 = (bf16[33,336,128]{2,1,0:T(8,128)(2,1)S(1)}, bf16[33,336,128]{2,1,0:T(8,128)(2,1)}, u32[]{:S(2)}, u32[]{:S(2)}) collective-permute-start(bf16[33,336,128]{2,1,0:T(8,128)(2,1)S(1)} %get-tuple-element.37), channel_id=1, source_target_pairs={{0,8},{1,9},{2,10},{3,11},{4,100},{5,101},{6,102},{7,103},{8,0},{9... | collective-permute-start | bytes 8515592 | tf_op jit(solution)/shard_map/ppermute | solution.py:348
  164.7 45.3 %collective-permute-start.21 = (bf16[33,352,128]{2,1,0:T(8,128)(2,1)S(1)}, bf16[33,352,128]{2,1,0:T(8,128)(2,1)S(1)}, u32[]{:S(2)}, u32[]{:S(2)}) collective-permute-start(bf16[33,352,128]{2,1,0:T(8,128)(2,1)S(1)} %get-tuple-element.35), channel_id=1, source_target_pairs={{0,1},{1,0},{2,3},{3,2},{4,28},{5,29},{6,30},{7,31},{8,9},{9,8},{1... | collective-permute-start | bytes 8921096 | tf_op jit(solution)/shard_map/ppermute | solution.py:348
  177.0 33.8 %collective-permute-start.34 = (bf16[16,336,128]{2,1,0:T(8,128)(2,1)S(1)}, bf16[16,336,128]{2,1,0:T(8,128)(2,1)S(1)}, u32[]{:S(2)}, u32[]{:S(2)}) collective-permute-start(bf16[16,336,128]{2,1,0:T(8,128)(2,1)S(1)} %get-tuple-element.45), channel_id=1, source_target_pairs={{0,3},{1,2},{2,1},{3,0},{4,12},{5,13},{6,14},{7,15},{8,11},{9,10},... | collective-permute-start | bytes 4128776 | tf_op jit(solution)/shard_map/ppermute | solution.py:348
  200.3 27.0 %collective-permute-start.28 = (bf16[16,336,128]{2,1,0:T(8,128)(2,1)S(1)}, bf16[16,336,128]{2,1,0:T(8,128)(2,1)S(1)}, u32[]{:S(2)}, u32[]{:S(2)}) collective-permute-start(bf16[16,336,128]{2,1,0:T(8,128)(2,1)S(1)} %get-tuple-element.43), channel_id=1, source_target_pairs={{0,96},{1,97},{2,98},{3,99},{4,5},{5,4},{6,7},{7,6},{8,104},{9,105... | collective-permute-start | bytes 4128776 | tf_op jit(solution)/shard_map/ppermute | solution.py:348
  210.7 27.7 %collective-permute-start.22 = (bf16[16,352,128]{2,1,0:T(8,128)(2,1)S(1)}, bf16[16,352,128]{2,1,0:T(8,128)(2,1)S(1)}, u32[]{:S(2)}, u32[]{:S(2)}) collective-permute-start(bf16[16,352,128]{2,1,0:T(8,128)(2,1)S(1)} %get-tuple-element.41), channel_id=1, source_target_pairs={{0,24},{1,25},{2,26},{3,27},{4,36},{5,37},{6,38},{7,39},{8,16},{9,... | collective-permute-start | bytes 4325384 | tf_op jit(solution)/shard_map/ppermute | solution.py:348
  212.1 28.7 %collective-permute-start.35 = (bf16[8,336,128]{2,1,0:T(8,128)(2,1)}, bf16[8,336,128]{2,1,0:T(8,128)(2,1)}, u32[]{:S(2)}, u32[]{:S(2)}) collective-permute-start(bf16[8,336,128]{2,1,0:T(8,128)(2,1)} %get-tuple-element.51), channel_id=1, source_target_pairs={{0,8},{1,9},{2,10},{3,11},{4,100},{5,101},{6,102},{7,103},{8,0},{9... | collective-permute-start | bytes 2064392 | tf_op jit(solution)/shard_map/ppermute | solution.py:348
  228.5 13.7 %collective-permute-start.29 = (bf16[8,336,128]{2,1,0:T(8,128)(2,1)}, bf16[8,336,128]{2,1,0:T(8,128)(2,1)}, u32[]{:S(2)}, u32[]{:S(2)}) collective-permute-start(bf16[8,336,128]{2,1,0:T(8,128)(2,1)} %get-tuple-element.49), channel_id=1, source_target_pairs={{0,1},{1,0},{2,3},{3,2},{4,28},{5,29},{6,30},{7,31},{8,9},{9,8},{1... | collective-permute-start | bytes 2064392 | tf_op jit(solution)/shard_map/ppermute | solution.py:348
  238.8 13.0 %collective-permute-start.23 = (bf16[8,352,128]{2,1,0:T(8,128)(2,1)S(1)}, bf16[8,352,128]{2,1,0:T(8,128)(2,1)S(1)}, u32[]{:S(2)}, u32[]{:S(2)}) collective-permute-start(bf16[8,352,128]{2,1,0:T(8,128)(2,1)S(1)} %get-tuple-element.47), channel_id=1, source_target_pairs={{0,32},{1,33},{2,34},{3,35},{4,7},{5,6},{6,5},{7,4},{8,40},{9,41},... | collective-permute-start | bytes 2162696 | tf_op jit(solution)/shard_map/ppermute | solution.py:348
  242.1 10.5 %collective-permute-start.36 = (bf16[4,336,128]{2,1,0:T(8,128)(2,1)S(1)}, bf16[4,336,128]{2,1,0:T(8,128)(2,1)S(1)}, u32[]{:S(2)}, u32[]{:S(2)}) collective-permute-start(bf16[4,336,128]{2,1,0:T(8,128)(2,1)S(1)} %get-tuple-element.61), channel_id=1, source_target_pairs={{0,96},{1,97},{2,98},{3,99},{4,5},{5,4},{6,7},{7,6},{8,104},{9,105... | collective-permute-start | bytes 1032200 | tf_op jit(solution)/shard_map/ppermute | solution.py:348
  243.5 9.5 %collective-permute-start.30 = (bf16[4,336,128]{2,1,0:T(8,128)(2,1)S(1)}, bf16[4,336,128]{2,1,0:T(8,128)(2,1)S(1)}, u32[]{:S(2)}, u32[]{:S(2)}) collective-permute-start(bf16[4,336,128]{2,1,0:T(8,128)(2,1)S(1)} %get-tuple-element.59), channel_id=1, source_target_pairs={{0,24},{1,25},{2,26},{3,27},{4,36},{5,37},{6,38},{7,39},{8,16},{9,... | collective-permute-start | bytes 1032200 | tf_op jit(solution)/shard_map/ppermute | solution.py:348
  252.0 10.4 %collective-permute-start.24 = (bf16[4,352,128]{2,1,0:T(8,128)(2,1)S(1)}, bf16[4,352,128]{2,1,0:T(8,128)(2,1)S(1)}, u32[]{:S(2)}, u32[]{:S(2)}) collective-permute-start(bf16[4,352,128]{2,1,0:T(8,128)(2,1)S(1)} %get-tuple-element.57), channel_id=1, source_target_pairs={{0,3},{1,2},{2,1},{3,0},{4,12},{5,13},{6,14},{7,15},{8,11},{9,10},... | collective-permute-start | bytes 1081352 | tf_op jit(solution)/shard_map/ppermute | solution.py:348
  252.6 5.5 %collective-permute-start.37 = (bf16[2,336,128]{2,1,0:T(8,128)(2,1)S(1)}, bf16[2,336,128]{2,1,0:T(8,128)(2,1)S(1)}, u32[]{:S(2)}, u32[]{:S(2)}) collective-permute-start(bf16[2,336,128]{2,1,0:T(8,128)(2,1)S(1)} %get-tuple-element.67), channel_id=1, source_target_pairs={{0,1},{1,0},{2,3},{3,2},{4,28},{5,29},{6,30},{7,31},{8,9},{9,8},{1... | collective-permute-start | bytes 516104 | tf_op jit(solution)/shard_map/ppermute | solution.py:348
  253.0 5.5 %collective-permute-start.31 = (bf16[2,336,128]{2,1,0:T(8,128)(2,1)S(1)}, bf16[2,336,128]{2,1,0:T(8,128)(2,1)S(1)}, u32[]{:S(2)}, u32[]{:S(2)}) collective-permute-start(bf16[2,336,128]{2,1,0:T(8,128)(2,1)S(1)} %get-tuple-element.65), channel_id=1, source_target_pairs={{0,32},{1,33},{2,34},{3,35},{4,7},{5,6},{6,5},{7,4},{8,40},{9,41},... | collective-permute-start | bytes 516104 | tf_op jit(solution)/shard_map/ppermute | solution.py:348
  258.1 15.8 %copy-start.1 = (bf16[128,1024]{1,0:T(8,128)(2,1)S(1)}, bf16[128,1024]{1,0:T(8,128)(2,1)}, u32[]{:S(2)}) copy-start(bf16[128,1024]{1,0:T(8,128)(2,1)} %param.13) | copy-start | bytes 786436
  258.2 5.8 %collective-permute-start.38 = (bf16[1,336,128]{2,1,0:T(8,128)(2,1)S(1)}, bf16[1,336,128]{2,1,0:T(8,128)(2,1)S(1)}, u32[]{:S(2)}, u32[]{:S(2)}) collective-permute-start(bf16[1,336,128]{2,1,0:T(8,128)(2,1)S(1)} %add_convert_fusion.26), channel_id=1, source_target_pairs={{0,24},{1,25},{2,26},{3,27},{4,36},{5,37},{6,38},{7,39},{8,16},{9,... | collective-permute-start | bytes 258056 | tf_op jit(solution)/shard_map/ppermute | solution.py:348
  258.6 10.3 %collective-permute-start.32 = (bf16[1,336,128]{2,1,0:T(8,128)(2,1)S(1)}, bf16[1,336,128]{2,1,0:T(8,128)(2,1)S(1)}, u32[]{:S(2)}, u32[]{:S(2)}) collective-permute-start(bf16[1,336,128]{2,1,0:T(8,128)(2,1)S(1)} %add_convert_fusion.28), channel_id=1, source_target_pairs={{0,3},{1,2},{2,1},{3,0},{4,12},{5,13},{6,14},{7,15},{8,11},{9,10},... | collective-permute-start | bytes 258056 | tf_op jit(solution)/shard_map/ppermute | solution.py:348
  262.4 15.8 %copy-start = (bf16[4096,256]{1,0:T(8,128)(2,1)S(1)}, bf16[4096,256]{1,0:T(8,128)(2,1)}, u32[]{:S(2)}) copy-start(bf16[4096,256]{1,0:T(8,128)(2,1)} %param.21) | copy-start | bytes 6291460
  262.5 5.6 %collective-permute-start.25 = (bf16[2,352,128]{2,1,0:T(8,128)(2,1)S(1)}, bf16[2,352,128]{2,1,0:T(8,128)(2,1)S(1)}, u32[]{:S(2)}, u32[]{:S(2)}) collective-permute-start(bf16[2,352,128]{2,1,0:T(8,128)(2,1)S(1)} %get-tuple-element.63), channel_id=1, source_target_pairs={{0,8},{1,9},{2,10},{3,11},{4,100},{5,101},{6,102},{7,103},{8,0},{9... | collective-permute-start | bytes 540680 | tf_op jit(solution)/shard_map/ppermute | solution.py:348
  268.1 5.8 %collective-permute-start.26 = (bf16[1,352,128]{2,1,0:T(8,128)(2,1)S(1)}, bf16[1,352,128]{2,1,0:T(8,128)(2,1)S(1)}, u32[]{:S(2)}, u32[]{:S(2)}) collective-permute-start(bf16[1,352,128]{2,1,0:T(8,128)(2,1)S(1)} %add_convert_fusion.24), channel_id=1, source_target_pairs={{0,96},{1,97},{2,98},{3,99},{4,5},{5,4},{6,7},{7,6},{8,104},{9,105... | collective-permute-start | bytes 270344 | tf_op jit(solution)/shard_map/ppermute | solution.py:348
  274.0 11.7 %copy-start.2 = (bf16[128,1024]{1,0:T(8,128)(2,1)}, bf16[128,1024]{1,0:T(8,128)(2,1)S(1)}, u32[]{:S(2)}) copy-start(bf16[128,1024]{1,0:T(8,128)(2,1)S(1)} %fusion.19) | copy-start | bytes 786436
  274.0 10.5 %collective-permute-start.41 = (bf16[128,1024]{1,0:T(8,128)(2,1)S(1)}, bf16[128,1024]{1,0:T(8,128)(2,1)S(1)}, u32[]{:S(2)}, u32[]{:S(2)}) collective-permute-start(bf16[128,1024]{1,0:T(8,128)(2,1)S(1)} %fusion.19), channel_id=1, source_target_pairs={{0,3},{1,2},{2,1},{3,0},{4,7},{5,6},{6,5},{7,4},{8,11},{9,10},{10,... | collective-permute-start | bytes 786440 | tf_op jit(solution)/shard_map/ppermute | solution.py:381
  274.1 10.4 %collective-permute-start.40 = (bf16[128,1024]{1,0:T(8,128)(2,1)S(1)}, bf16[128,1024]{1,0:T(8,128)(2,1)S(1)}, u32[]{:S(2)}, u32[]{:S(2)}) collective-permute-start(bf16[128,1024]{1,0:T(8,128)(2,1)S(1)} %fusion.19), channel_id=1, source_target_pairs={{0,2},{1,3},{2,0},{3,1},{4,6},{5,7},{6,4},{7,5},{8,10},{9,11},{10,... | collective-permute-start | bytes 786440 | tf_op jit(solution)/shard_map/ppermute | solution.py:381
  276.4 8.9 %collective-permute-start.39 = (bf16[128,1024]{1,0:T(8,128)(2,1)S(1)}, bf16[128,1024]{1,0:T(8,128)(2,1)S(1)}, u32[]{:S(2)}, u32[]{:S(2)}) collective-permute-start(bf16[128,1024]{1,0:T(8,128)(2,1)S(1)} %fusion.19), channel_id=1, source_target_pairs={{0,1},{1,0},{2,3},{3,2},{4,5},{5,4},{6,7},{7,6},{8,9},{9,8},{10,11... | collective-permute-start | bytes 786440 | tf_op jit(solution)/shard_map/ppermute | solution.py:381
  (7 other events, 30.2 us)
